TPU v7x, 256 devices: a whole 4x4x8 slice. The times are simulated.
256 devices in a mesh: grid: 16 (over z, x_lo), sta: 16 (over y, x_hi, core).
Axes of the slice: x: 4 (x_hi: 2, x_lo: 2; x = x_hi * 2 + x_lo), y: 4, z: 8, core: 2. Of those that a mesh axis runs over, the one named last changes fastest.
Arguments:
- u_now: float32 [2048, 4096], P('grid', 'sta'), may hold values from -6 to 6
- u_prev: float32 [2048, 4096], P('grid', 'sta'), may hold values from -6 to 6
- buoyancy: float32 [2048, 4096], P('grid', 'sta'), may hold values from 0.5 to 1
- modulus: float32 [2048, 4096], P('grid', 'sta'), may hold values from 0.2 to 0.45
- station_cell: int32 [32768], P(('grid', 'sta')), may hold values from 0 to 8388607, as said below
- path_class: int32 [32768, 2048], P(('grid', 'sta')), may hold values from 0 to 7
- spectra: bfloat16 [2048, 512], P('sta'), may hold values from 0.099609375 to 1
- cos_table: float32 [2048, 512], P('sta')
- sin_table: float32 [2048, 512], P('sta')
- path_filter: float32 [8, 512], replicated, may hold values from 0.1 to 2
- lf_basis: float32 [4, 1024], replicated, may hold values from -3 to 3
- crossover: float32 [512], replicated, may hold values from 0.05 to 0.95
Outputs:
- broadband: float32 [32768, 1024], P(('grid', 'sta'))
- u_final: float32 [2048, 4096], P('grid', 'sta')
Inputs may be any that keep to these rules, and one draw needn't show every extreme that they name: `station_cell`: station i lies in the columns of grid block ((i // 128) % 16) along the second dimension; its cell is row * 4096 + column.
All inputs are finite; a program needn't handle non-finite values.
Results may differ from a plain program's by a relative error of at most 0.0033.
Values may be sent and summed in bfloat16 or wider, within the bound.
A program may use at most 64 MiB of HBM per device.

v0:
```python
import jax
import jax.numpy as jnp
from jax import lax
from jax.sharding import PartitionSpec as P

STEPS = 4
CLASSES = 8


def extended(block, sides, width):
    for axis, dim in sides:
        count = lax.axis_size(axis)
        forward = [(i, i + 1) for i in range(count - 1)]
        backward = [(target, source) for source, target in forward]
        low = lax.ppermute(
            lax.slice_in_dim(block, block.shape[dim] - width, None, axis=dim), axis, forward
        )
        high = lax.ppermute(lax.slice_in_dim(block, 0, width, axis=dim), axis, backward)
        block = jnp.concatenate([low, block, high], axis=dim)
    return block


def divergence(padu, padm):
    center = padu[1:-1, 1:-1]
    mid = padm[1:-1, 1:-1]
    right = 0.5 * (mid + padm[2:, 1:-1]) * (padu[2:, 1:-1] - center)
    left = 0.5 * (mid + padm[:-2, 1:-1]) * (center - padu[:-2, 1:-1])
    upper = 0.5 * (mid + padm[1:-1, 2:]) * (padu[1:-1, 2:] - center)
    lower = 0.5 * (mid + padm[1:-1, :-2]) * (center - padu[1:-1, :-2])
    return right - left + upper - lower


def onehot_rows(classes):
    levels = jnp.arange(CLASSES, dtype=jnp.int32)
    onehot = (classes[:, :, None] == levels[None, None, :]).astype(jnp.bfloat16)
    return onehot.reshape(classes.shape[0], classes.shape[1] * CLASSES)


def expand_terms(piece, doubled):
    terms = (piece.astype(jnp.float32)[:, None, :] * doubled[None, :, :]).astype(jnp.bfloat16)
    return terms.reshape(piece.shape[0] * CLASSES, doubled.shape[1])


def merging(low, high, crossover):
    lowpass = jnp.concatenate([crossover, crossover])[None, :]
    weight = lowpass * (1.0 - lowpass)
    numer = jnp.mean(weight * low * low, axis=1)
    denom = jnp.mean(weight * high * high, axis=1)
    ratio = jnp.sqrt((numer + 1e-06) / (denom + 1e-06))
    return lowpass * low + (1.0 - lowpass) * ratio[:, None] * high


def local(
    u_now,
    u_prev,
    buoyancy,
    modulus,
    station_cell,
    path_class,
    spectra,
    cos_table,
    sin_table,
    path_filter,
    lf_basis,
    crossover,
):
    rows_local, cols_local = u_now.shape
    grid_pos = lax.axis_index("grid")
    sta_pos = lax.axis_index("sta")
    full_cols = cols_local * lax.axis_size("sta")
    column_cells = lax.all_gather(station_cell, "grid", axis=0, tiled=True)
    row_of = column_cells // full_cols - grid_pos * rows_local
    col_of = column_cells % full_cols - sta_pos * cols_local
    inside = (row_of >= 0) & (row_of < rows_local)
    flat_index = jnp.where(inside, row_of * cols_local + col_of, 0)
    present = inside.astype(jnp.float32)
    recorded = []
    padm = extended(modulus, (("grid", 0), ("sta", 1)), 1)
    current, previous = (u_now, u_prev)
    for step in range(STEPS):
        padu = extended(current, (("grid", 0), ("sta", 1)), 1)
        following = 2.0 * current - previous + buoyancy * divergence(padu, padm)
        previous, current = (current, following)
        recorded.append(jnp.take(current.reshape(-1), flat_index) * present)
    samples = lax.psum_scatter(jnp.stack(recorded), "grid", scatter_dimension=1, tiled=True)
    low = jnp.dot(
        samples.T, lf_basis, precision=lax.Precision.HIGHEST, preferred_element_type=jnp.float32
    )
    wide = spectra.astype(jnp.float32)
    phased = jnp.concatenate([wide * cos_table, wide * sin_table], axis=1).astype(jnp.bfloat16)
    doubled = jnp.concatenate([path_filter, path_filter], axis=1)
    high = jnp.dot(
        onehot_rows(path_class),
        expand_terms(lax.all_gather(phased, "sta", axis=0, tiled=True), doubled),
        preferred_element_type=jnp.float32,
    )
    return (merging(low, high, crossover), current)


def solution(mesh):
    in_specs = (
        P("grid", "sta"),
        P("grid", "sta"),
        P("grid", "sta"),
        P("grid", "sta"),
        P(("grid", "sta")),
        P(("grid", "sta"), None),
        P("sta", None),
        P("sta", None),
        P("sta", None),
        P(),
        P(),
        P(),
    )
    out_specs = (P(("grid", "sta"), None), P("grid", "sta"))
    return jax.shard_map(local, mesh=mesh, in_specs=in_specs, out_specs=out_specs, check_vma=False)
```

profile of v0, /device:TPU:8, one launch (start us, length us, event | category | flops | bytes accessed | tf_op | source)
XLA Modules:
  0.0 268.3 jit_solution(1673130394665267363)
XLA Ops:
  8.0 0.0 all-gather.3.cloned.1.call-start
  8.1 1.2 fusion.7
  9.2 0.7 pad_maximum_fusion
  9.9 0.0 all-gather.3.cloned.1.call-update
  10.0 0.0 reduce-scatter.4.cloned.1.call-start
  10.0 0.7 fusion.88
  10.7 1.3 collective-permute-start.1
  12.0 4.5 %collective-permute-start.3 = (f32[1,256]{1,0:T(1,128)S(1)}, f32[1,256]{1,0:T(1,128)S(1)}, u32[]{:S(2)}, u32[]{:S(2)}) collective-permute-start(f32[1,256]{1,0:T(1,128)S(1)} %get-tuple-element.28), channel_id=1, source_target_pairs={{0,16},{16,32},{32,48},{48,64},{64,80},{80,96},{96,112},{112,128},... | collective-permute-start | bytes 3080 | tf_op jit(solution)/shard_map/ppermute | solution.py:15
  16.6 0.7 fusion.87
  17.3 1.3 collective-permute-start
  18.6 4.9 %collective-permute-start.2 = (f32[1,256]{1,0:T(1,128)S(1)}, f32[1,256]{1,0:T(1,128)S(1)}, u32[]{:S(2)}, u32[]{:S(2)}) collective-permute-start(f32[1,256]{1,0:T(1,128)S(1)} %get-tuple-element.26), channel_id=1, source_target_pairs={{0,16},{16,32},{32,48},{48,64},{64,80},{80,96},{96,112},{112,128},... | collective-permute-start | bytes 3080 | tf_op jit(solution)/shard_map/ppermute | solution.py:15
  23.5 36.0 %all-gather = s32[16,1,128]{2,1,0:T(1,128)S(1)} all-gather(s32[1,1,128]{2,1,0:T(1,128)} %bitcast.37), channel_id=1, replica_groups=mesh['grid'=16,'sta'=16] {'grid'}, dimensions={0}, use_global_device_ids=true | all-gather | bytes 8704 | tf_op jit(solution)/shard_map/all_gather | solution.py:71
  59.5 0.9 pad_maximum_fusion.2
  60.5 0.1 fusion.83
  60.5 1.9 collective-permute-start.7
  62.5 6.0 %collective-permute-start.5 = (f32[130,1]{1,0:T(8,128)S(1)}, f32[130,1]{1,0:T(8,128)S(1)}, u32[]{:S(2)}, u32[]{:S(2)}) collective-permute-start(f32[130,1]{1,0:T(8,128)S(1)} %get-tuple-element.18), channel_id=1, source_target_pairs={{1,0},{2,1},{3,2},{4,3},{5,4},{6,5},{7,6},{8,7},{9,8},{10,9},{11,1... | collective-permute-start | bytes 1568 | tf_op jit(solution)/shard_map/ppermute | solution.py:18
  68.5 0.9 pad_maximum_fusion.1
  69.5 0.1 fusion.82
  69.5 1.9 collective-permute-start.4
  71.5 2.4 collective-permute-start.6
  73.9 5.6 %collective-permute-done.6 = f32[130,1]{1,0:T(8,128)S(1)} collective-permute-done((f32[130,1]{1,0:T(8,128)S(1)}, f32[130,1]{1,0:T(8,128)S(1)}, u32[]{:S(2)}, u32[]{:S(2)}) %collective-permute-start.6) | collective-permute-done | bytes 552 | tf_op jit(solution)/shard_map/ppermute | solution.py:15
  79.5 1.8 fusion.52
  81.3 1.3 collective-permute-start.8
  82.6 4.5 %collective-permute-start.9 = (f32[1,256]{1,0:T(1,128)S(1)}, f32[1,256]{1,0:T(1,128)S(1)}, u32[]{:S(2)}, u32[]{:S(2)}) collective-permute-start(f32[1,256]{1,0:T(1,128)S(1)} %get-tuple-element.24), channel_id=1, source_target_pairs={{0,16},{16,32},{32,48},{48,64},{64,80},{80,96},{96,112},{112,128},... | collective-permute-start | bytes 3080 | tf_op jit(solution)/shard_map/ppermute | solution.py:15
  87.2 1.2 collective-permute-done.9
  88.4 0.1 fusion.81
  88.5 1.9 collective-permute-start.11
  90.4 6.0 %collective-permute-start.10 = (f32[130,1]{1,0:T(8,128)S(1)}, f32[130,1]{1,0:T(8,128)S(1)}, u32[]{:S(2)}, u32[]{:S(2)}) collective-permute-start(f32[130,1]{1,0:T(8,128)S(1)} %get-tuple-element.14), channel_id=1, source_target_pairs={{1,0},{2,1},{3,2},{4,3},{5,4},{6,5},{7,6},{8,7},{9,8},{10,9},{11,1... | collective-permute-start | bytes 1568 | tf_op jit(solution)/shard_map/ppermute | solution.py:18
  96.5 0.7 constant_dynamic-update-slice_fusion.1
  97.2 1.2 collective-permute-done.10
  98.4 1.5 fusion.39
  100.0 1.3 collective-permute-start.12
  101.3 4.8 %collective-permute-start.13 = (f32[1,256]{1,0:T(1,128)S(1)}, f32[1,256]{1,0:T(1,128)S(1)}, u32[]{:S(2)}, u32[]{:S(2)}) collective-permute-start(f32[1,256]{1,0:T(1,128)S(1)} %get-tuple-element.22), channel_id=1, source_target_pairs={{0,16},{16,32},{32,48},{48,64},{64,80},{80,96},{96,112},{112,128},... | collective-permute-start | bytes 3080 | tf_op jit(solution)/shard_map/ppermute | solution.py:15
  106.1 0.7 constant_dynamic-update-slice_fusion
  106.8 0.6 collective-permute-done.13
  107.4 0.1 fusion.80
  107.4 1.9 collective-permute-start.15
  109.4 6.0 %collective-permute-start.14 = (f32[130,1]{1,0:T(8,128)S(1)}, f32[130,1]{1,0:T(8,128)S(1)}, u32[]{:S(2)}, u32[]{:S(2)}) collective-permute-start(f32[130,1]{1,0:T(8,128)S(1)} %get-tuple-element.12), channel_id=1, source_target_pairs={{1,0},{2,1},{3,2},{4,3},{5,4},{6,5},{7,6},{8,7},{9,8},{10,9},{11,1... | collective-permute-start | bytes 1568 | tf_op jit(solution)/shard_map/ppermute | solution.py:18
  115.4 0.0 collective-permute-done.15
  115.5 1.9 collective-permute-done.14
  117.3 1.5 fusion.26
  118.8 1.3 collective-permute-start.16
  120.1 5.4 %collective-permute-start.17 = (f32[1,256]{1,0:T(1,128)S(1)}, f32[1,256]{1,0:T(1,128)S(1)}, u32[]{:S(2)}, u32[]{:S(2)}) collective-permute-start(f32[1,256]{1,0:T(1,128)S(1)} %get-tuple-element.20), channel_id=1, source_target_pairs={{0,16},{16,32},{32,48},{48,64},{64,80},{80,96},{96,112},{112,128},... | collective-permute-start | bytes 3080 | tf_op jit(solution)/shard_map/ppermute | solution.py:15
  125.6 0.8 pad_maximum_fusion.47
  126.4 0.1 copy.16
  126.5 11.8 %gather_fusion = f32[2048]{0:T(1024)S(1)} fusion(f32[32768]{0:T(1024)S(1)} %bitcast.23, s32[2048]{0:T(1024)S(1)} %get-tuple-element.7), kind=kCustom, calls=%fused_computation.clone | custom fusion | bytes 24576 | tf_op jit(solution)/shard_map/jit(_take)/gather | solution.py:84
  138.3 0.1 fusion.79
  138.4 1.9 collective-permute-start.19
  140.3 6.6 %collective-permute-start.18 = (f32[130,1]{1,0:T(8,128)S(1)}, f32[130,1]{1,0:T(8,128)S(1)}, u32[]{:S(2)}, u32[]{:S(2)}) collective-permute-start(f32[130,1]{1,0:T(8,128)S(1)} %get-tuple-element.10), channel_id=1, source_target_pairs={{1,0},{2,1},{3,2},{4,3},{5,4},{6,5},{7,6},{8,7},{9,8},{10,9},{11,1... | collective-permute-start | bytes 1568 | tf_op jit(solution)/shard_map/ppermute | solution.py:18
  146.9 0.1 copy.17
  147.0 11.8 %gather_fusion.1 = f32[2048]{0:T(1024)S(1)} fusion(f32[32768]{0:T(1024)S(1)} %bitcast.25, s32[2048]{0:T(1024)S(1)} %get-tuple-element.7), kind=kCustom, calls=%fused_computation.1.clone | custom fusion | bytes 24576 | tf_op jit(solution)/shard_map/jit(_take)/gather | solution.py:84
  158.8 0.1 copy.18
  158.9 11.8 %gather_fusion.2 = f32[2048]{0:T(1024)S(1)} fusion(f32[32768]{0:T(1024)S(1)} %bitcast.26, s32[2048]{0:T(1024)S(1)} %get-tuple-element.7), kind=kCustom, calls=%fused_computation.2.clone | custom fusion | bytes 24576 | tf_op jit(solution)/shard_map/jit(_take)/gather | solution.py:84
  170.7 0.3 fusion.13
  171.0 0.1 copy.19
  171.1 11.8 %gather_fusion.3 = f32[2048]{0:T(1024)S(1)} fusion(f32[32768]{0:T(1024)S(1)} %bitcast.24, s32[2048]{0:T(1024)S(1)} %get-tuple-element.7), kind=kCustom, calls=%fused_computation.3.clone | custom fusion | bytes 24576 | tf_op jit(solution)/shard_map/jit(_take)/gather | solution.py:84
  183.0 1.3 copy.14
  184.3 0.0 reduce-scatter.4.cloned.1.call-update
  184.3 0.0 all-gather.3.cloned.1.call-done
  184.4 6.5 %convert_element_type.13 = f32[2048,1024]{1,0:T(8,128)} convert(bf16[2048,1024]{1,0:T(8,128)(2,1)} %all-gather.3.cloned.1.call-done) | non-fusion elementwise | flops 2097152 | bytes 12582912 | tf_op jit(solution)/shard_map/convert_element_type | solution.py:40
  190.9 8.5 %fusion.4 = f32[128,1024]{1,0:T(8,128)S(1)} fusion(f32[8,1024]{1,0:T(8,128)S(1)} %pad_maximum_fusion.47, f32[2048,1024]{1,0:T(8,128)} %convert_element_type.13, s32[128,2048]{1,0:T(8,128)S(1)} %copy-done.4), kind=kOutput, calls=%fused_computation.10 | convolution fusion | flops 4330618880 | bytes 9994240 | tf_op jit(solution)/shard_map/dot_general | solution.py:92
  199.4 59.0 %reduce-scatter.4.cloned.1.call-done = f32[128,4]{1,0:T(8,128)} async-done(((f32[2048,4]{1,0:T(8,128)}), f32[128,4]{1,0:T(8,128)}) %reduce-scatter.4.cloned.1.call-update) | async-done | bytes 2064
  258.4 1.5 fusion.5
  259.9 0.9 multiply_add_fusion
  (37 shorter events, 0.2 us)
Async XLA Ops:
  8.0 250.4 %copy-start = (f32[4,1024]{1,0:T(4,128)S(1)}, f32[4,1024]{1,0:T(4,128)}, u32[]{:S(2)}) copy-start(f32[4,1024]{1,0:T(4,128)} %param.24) | copy-start | bytes 49156
  8.0 176.3 %all-gather.3.cloned.1.call-start = ((), (), s32[]{:S(2)}) async-start(), calls=%async_computation.1 | async-start | bytes 4456448 | tf_op jit(solution)/shard_map/all_gather | solution.py:94
  10.0 248.4 %reduce-scatter.4.cloned.1.call-start = ((), (), s32[]{:S(2)}) async-start(), calls=%async_computation.2 | async-start | bytes 1114112
  10.7 48.8 %collective-permute-start.1 = (f32[1,256]{1,0:T(1,128)S(1)}, f32[1,256]{1,0:T(1,128)S(1)}, u32[]{:S(2)}, u32[]{:S(2)}) collective-permute-start(f32[1,256]{1,0:T(1,128)S(1)} %get-tuple-element.29), channel_id=1, source_target_pairs={{16,0},{32,16},{48,32},{64,48},{80,64},{96,80},{112,96},{128,112},... | collective-permute-start | bytes 3080 | tf_op jit(solution)/shard_map/ppermute | solution.py:18
  12.0 47.5 %collective-permute-start.3 = (f32[1,256]{1,0:T(1,128)S(1)}, f32[1,256]{1,0:T(1,128)S(1)}, u32[]{:S(2)}, u32[]{:S(2)}) collective-permute-start(f32[1,256]{1,0:T(1,128)S(1)} %get-tuple-element.28), channel_id=1, source_target_pairs={{0,16},{16,32},{32,48},{48,64},{64,80},{80,96},{96,112},{112,128},... | collective-permute-start | bytes 3080 | tf_op jit(solution)/shard_map/ppermute | solution.py:15
  17.3 51.2 %collective-permute-start = (f32[1,256]{1,0:T(1,128)S(1)}, f32[1,256]{1,0:T(1,128)S(1)}, u32[]{:S(2)}, u32[]{:S(2)}) collective-permute-start(f32[1,256]{1,0:T(1,128)S(1)} %get-tuple-element.27), channel_id=1, source_target_pairs={{16,0},{32,16},{48,32},{64,48},{80,64},{96,80},{112,96},{128,112},... | collective-permute-start | bytes 3080 | tf_op jit(solution)/shard_map/ppermute | solution.py:18
  18.6 49.9 %collective-permute-start.2 = (f32[1,256]{1,0:T(1,128)S(1)}, f32[1,256]{1,0:T(1,128)S(1)}, u32[]{:S(2)}, u32[]{:S(2)}) collective-permute-start(f32[1,256]{1,0:T(1,128)S(1)} %get-tuple-element.26), channel_id=1, source_target_pairs={{0,16},{16,32},{32,48},{48,64},{64,80},{80,96},{96,112},{112,128},... | collective-permute-start | bytes 3080 | tf_op jit(solution)/shard_map/ppermute | solution.py:15
  60.5 13.4 %collective-permute-start.7 = (f32[130,1]{1,0:T(8,128)S(1)}, f32[130,1]{1,0:T(8,128)S(1)}, u32[]{:S(2)}, u32[]{:S(2)}) collective-permute-start(f32[130,1]{1,0:T(8,128)S(1)} %get-tuple-element.19), channel_id=1, source_target_pairs={{0,1},{1,2},{2,3},{3,4},{4,5},{5,6},{6,7},{7,8},{8,9},{9,10},{10,1... | collective-permute-start | bytes 1568 | tf_op jit(solution)/shard_map/ppermute | solution.py:15
  62.5 11.4 %collective-permute-start.5 = (f32[130,1]{1,0:T(8,128)S(1)}, f32[130,1]{1,0:T(8,128)S(1)}, u32[]{:S(2)}, u32[]{:S(2)}) collective-permute-start(f32[130,1]{1,0:T(8,128)S(1)} %get-tuple-element.18), channel_id=1, source_target_pairs={{1,0},{2,1},{3,2},{4,3},{5,4},{6,5},{7,6},{8,7},{9,8},{10,9},{11,1... | collective-permute-start | bytes 1568 | tf_op jit(solution)/shard_map/ppermute | solution.py:18
  69.5 4.4 %collective-permute-start.4 = (f32[130,1]{1,0:T(8,128)S(1)}, f32[130,1]{1,0:T(8,128)S(1)}, u32[]{:S(2)}, u32[]{:S(2)}) collective-permute-start(f32[130,1]{1,0:T(8,128)S(1)} %get-tuple-element.17), channel_id=1, source_target_pairs={{1,0},{2,1},{3,2},{4,3},{5,4},{6,5},{7,6},{8,7},{9,8},{10,9},{11,1... | collective-permute-start | bytes 1568 | tf_op jit(solution)/shard_map/ppermute | solution.py:18
  71.5 8.0 %collective-permute-start.6 = (f32[130,1]{1,0:T(8,128)S(1)}, f32[130,1]{1,0:T(8,128)S(1)}, u32[]{:S(2)}, u32[]{:S(2)}) collective-permute-start(f32[130,1]{1,0:T(8,128)S(1)} %get-tuple-element.16), channel_id=1, source_target_pairs={{0,1},{1,2},{2,3},{3,4},{4,5},{5,6},{6,7},{7,8},{8,9},{9,10},{10,1... | collective-permute-start | bytes 1568 | tf_op jit(solution)/shard_map/ppermute | solution.py:15
  81.3 5.9 %collective-permute-start.8 = (f32[1,256]{1,0:T(1,128)S(1)}, f32[1,256]{1,0:T(1,128)S(1)}, u32[]{:S(2)}, u32[]{:S(2)}) collective-permute-start(f32[1,256]{1,0:T(1,128)S(1)} %get-tuple-element.25), channel_id=1, source_target_pairs={{16,0},{32,16},{48,32},{64,48},{80,64},{96,80},{112,96},{128,112},... | collective-permute-start | bytes 3080 | tf_op jit(solution)/shard_map/ppermute | solution.py:18
  82.6 5.8 %collective-permute-start.9 = (f32[1,256]{1,0:T(1,128)S(1)}, f32[1,256]{1,0:T(1,128)S(1)}, u32[]{:S(2)}, u32[]{:S(2)}) collective-permute-start(f32[1,256]{1,0:T(1,128)S(1)} %get-tuple-element.24), channel_id=1, source_target_pairs={{0,16},{16,32},{32,48},{48,64},{64,80},{80,96},{96,112},{112,128},... | collective-permute-start | bytes 3080 | tf_op jit(solution)/shard_map/ppermute | solution.py:15
  88.5 8.7 %collective-permute-start.11 = (f32[130,1]{1,0:T(8,128)S(1)}, f32[130,1]{1,0:T(8,128)S(1)}, u32[]{:S(2)}, u32[]{:S(2)}) collective-permute-start(f32[130,1]{1,0:T(8,128)S(1)} %get-tuple-element.15), channel_id=1, source_target_pairs={{0,1},{1,2},{2,3},{3,4},{4,5},{5,6},{6,7},{7,8},{8,9},{9,10},{10,1... | collective-permute-start | bytes 1568 | tf_op jit(solution)/shard_map/ppermute | solution.py:15
  90.4 8.0 %collective-permute-start.10 = (f32[130,1]{1,0:T(8,128)S(1)}, f32[130,1]{1,0:T(8,128)S(1)}, u32[]{:S(2)}, u32[]{:S(2)}) collective-permute-start(f32[130,1]{1,0:T(8,128)S(1)} %get-tuple-element.14), channel_id=1, source_target_pairs={{1,0},{2,1},{3,2},{4,3},{5,4},{6,5},{7,6},{8,7},{9,8},{10,9},{11,1... | collective-permute-start | bytes 1568 | tf_op jit(solution)/shard_map/ppermute | solution.py:18
  100.0 6.8 %collective-permute-start.12 = (f32[1,256]{1,0:T(1,128)S(1)}, f32[1,256]{1,0:T(1,128)S(1)}, u32[]{:S(2)}, u32[]{:S(2)}) collective-permute-start(f32[1,256]{1,0:T(1,128)S(1)} %get-tuple-element.23), channel_id=1, source_target_pairs={{16,0},{32,16},{48,32},{64,48},{80,64},{96,80},{112,96},{128,112},... | collective-permute-start | bytes 3080 | tf_op jit(solution)/shard_map/ppermute | solution.py:18
  101.3 6.1 %collective-permute-start.13 = (f32[1,256]{1,0:T(1,128)S(1)}, f32[1,256]{1,0:T(1,128)S(1)}, u32[]{:S(2)}, u32[]{:S(2)}) collective-permute-start(f32[1,256]{1,0:T(1,128)S(1)} %get-tuple-element.22), channel_id=1, source_target_pairs={{0,16},{16,32},{32,48},{48,64},{64,80},{80,96},{96,112},{112,128},... | collective-permute-start | bytes 3080 | tf_op jit(solution)/shard_map/ppermute | solution.py:15
  107.4 8.0 %collective-permute-start.15 = (f32[130,1]{1,0:T(8,128)S(1)}, f32[130,1]{1,0:T(8,128)S(1)}, u32[]{:S(2)}, u32[]{:S(2)}) collective-permute-start(f32[130,1]{1,0:T(8,128)S(1)} %get-tuple-element.13), channel_id=1, source_target_pairs={{0,1},{1,2},{2,3},{3,4},{4,5},{5,6},{6,7},{7,8},{8,9},{9,10},{10,1... | collective-permute-start | bytes 1568 | tf_op jit(solution)/shard_map/ppermute | solution.py:15
  109.4 8.0 %collective-permute-start.14 = (f32[130,1]{1,0:T(8,128)S(1)}, f32[130,1]{1,0:T(8,128)S(1)}, u32[]{:S(2)}, u32[]{:S(2)}) collective-permute-start(f32[130,1]{1,0:T(8,128)S(1)} %get-tuple-element.12), channel_id=1, source_target_pairs={{1,0},{2,1},{3,2},{4,3},{5,4},{6,5},{7,6},{8,7},{9,8},{10,9},{11,1... | collective-permute-start | bytes 1568 | tf_op jit(solution)/shard_map/ppermute | solution.py:18
  118.8 19.4 %collective-permute-start.16 = (f32[1,256]{1,0:T(1,128)S(1)}, f32[1,256]{1,0:T(1,128)S(1)}, u32[]{:S(2)}, u32[]{:S(2)}) collective-permute-start(f32[1,256]{1,0:T(1,128)S(1)} %get-tuple-element.21), channel_id=1, source_target_pairs={{16,0},{32,16},{48,32},{64,48},{80,64},{96,80},{112,96},{128,112},... | collective-permute-start | bytes 3080 | tf_op jit(solution)/shard_map/ppermute | solution.py:18
  120.1 18.1 %collective-permute-start.17 = (f32[1,256]{1,0:T(1,128)S(1)}, f32[1,256]{1,0:T(1,128)S(1)}, u32[]{:S(2)}, u32[]{:S(2)}) collective-permute-start(f32[1,256]{1,0:T(1,128)S(1)} %get-tuple-element.20), channel_id=1, source_target_pairs={{0,16},{16,32},{32,48},{48,64},{64,80},{80,96},{96,112},{112,128},... | collective-permute-start | bytes 3080 | tf_op jit(solution)/shard_map/ppermute | solution.py:15
  138.4 32.3 %collective-permute-start.19 = (f32[130,1]{1,0:T(8,128)S(1)}, f32[130,1]{1,0:T(8,128)S(1)}, u32[]{:S(2)}, u32[]{:S(2)}) collective-permute-start(f32[130,1]{1,0:T(8,128)S(1)} %get-tuple-element.11), channel_id=1, source_target_pairs={{0,1},{1,2},{2,3},{3,4},{4,5},{5,6},{6,7},{7,8},{8,9},{9,10},{10,1... | collective-permute-start | bytes 1568 | tf_op jit(solution)/shard_map/ppermute | solution.py:15
  140.3 30.4 %collective-permute-start.18 = (f32[130,1]{1,0:T(8,128)S(1)}, f32[130,1]{1,0:T(8,128)S(1)}, u32[]{:S(2)}, u32[]{:S(2)}) collective-permute-start(f32[130,1]{1,0:T(8,128)S(1)} %get-tuple-element.10), channel_id=1, source_target_pairs={{1,0},{2,1},{3,2},{4,3},{5,4},{6,5},{7,6},{8,7},{9,8},{10,9},{11,1... | collective-permute-start | bytes 1568 | tf_op jit(solution)/shard_map/ppermute | solution.py:18
  147.0 23.7 %copy-start.1 = (f32[128,256]{1,0:T(8,128)S(1)}, f32[128,256]{1,0:T(8,128)}, u32[]{:S(2)}) copy-start(f32[128,256]{1,0:T(8,128)} %param.17) | copy-start | bytes 393220
  147.0 23.7 %copy-start.2 = (f32[128,256]{1,0:T(8,128)S(1)}, f32[128,256]{1,0:T(8,128)}, u32[]{:S(2)}) copy-start(f32[128,256]{1,0:T(8,128)} %param.16) | copy-start | bytes 393220
  171.0 19.9 %copy-start.3 = (f32[128,256]{1,0:T(8,128)}, f32[128,256]{1,0:T(8,128)S(1)}, u32[]{:S(2)}) copy-start(f32[128,256]{1,0:T(8,128)S(1)} %fusion.13) | copy-start | bytes 393220
  182.9 8.0 %copy-start.4 = (s32[128,2048]{1,0:T(8,128)S(1)}, s32[128,2048]{1,0:T(8,128)}, u32[]{:S(2)}) copy-start(s32[128,2048]{1,0:T(8,128)} %param.19) | copy-start | bytes 3145732
Sparse Core Ops, SparseCore 0:
  12.2 61.9 all-gather.2
Sparse Core Ops, SparseCore 1:
  184.4 73.9 reduce-scatter.3
where the time goes:
time: 269 us; the launch traced here: 268 us
  waiting for transfers between devices  69.6 us (26%)
  starting transfers between devices  67.5 us (25%)
  local copies, waits for them, and re-layouts  52 us (19%)
  blocking collectives  36 us (13%)
  other arithmetic  17.1 us (6%)
  between operations  16 us (6%)
  matrix products  10 us (4%)
    unnamed x3, waiting for transfers between devices  59 us
    gather x4, local copies, waits for them, and re-layouts, local(): recorded.append(jnp.take(current.reshape(-1), flat_index) * present)  47.1 us
    all_gather x1, blocking collectives, local(): column_cells = lax.all_gather(station_cell, 'grid', axis=0, tiled=True)  36 us
    ppermute x10, starting transfers between devices, extended(): lax.ppermute(lax.slice_in_dim(block, block.shape[dim] - width, None, axis...  34.3 us
    ppermute x10, starting transfers between devices, extended(): lax.ppermute(lax.slice_in_dim(block, 0, width, axis=dim), axis, backward)  33.1 us
    dot_general x1, matrix products, local(): jnp.dot(onehot_rows(path_class), expand_terms(lax.all_gather(phased, 'sta...  8.5 us
    ppermute x10, waiting for transfers between devices, extended(): lax.ppermute(lax.slice_in_dim(block, block.shape[dim] - width, None, axis...  7.45 us
    convert_element_type x1, other arithmetic, expand_terms(): piece.astype(jnp.float32)[:, None, :] * doubled[None, :, :]  6.51 us
  transfers between devices with their start and end apart: 22, of which 6 were waited for; matrix products, arithmetic and copies ran while one was open for 28% of the time, Pallas kernels for 0%

commit v1 on v0

v1 whole, which is shorter than its diff:
```python
import functools

import jax
import jax.numpy as jnp
from jax import lax
from jax.experimental import pallas as pl
from jax.experimental.pallas import tpu as pltpu
from jax.sharding import PartitionSpec as P

STEPS = 4
CLASSES = 8
MESH = pl.DeviceIdType.MESH
BF16 = jnp.bfloat16
F32 = jnp.float32

SLOTS = ((0, 0), (0, 1), (1, 0), (3, 0), (1, 1), (3, 1), (2, 0), (2, 1))
FAR = [(dy, cross, dc) for dy, cross in SLOTS[1:] for dc in (0, 1)]
HALO = [(-1, 0), (1, 0), (0, -1), (0, 1), (-1, -1), (-1, 1), (1, -1), (1, 1)]
GRID = 16
SUBCHIP = 256


def kernel(
    u_ref,
    up_ref,
    b_ref,
    m_ref,
    cell_ref,
    class_ref,
    spectra_ref,
    cos_ref,
    sin_ref,
    filter_ref,
    basis_ref,
    cross_ref,
    out_ref,
    ufinal_ref,
    cells,
    cellsrc,
    rowsrc,
    colsrc,
    rowin,
    colin,
    cornerin,
    ext,
    ush,
    sampsrc,
    sampin,
    classown,
    classsib,
    onehot,
    phased,
    pieces,
    high,
    highin,
    cell_send,
    cell_recv,
    halo_send,
    halo_recv,
    samp_send,
    samp_recv,
    far_send,
    far_recv,
    sib_send,
    sib_recv,
):
    g = lax.axis_index("grid")
    s = lax.axis_index("sta")
    z, xl = g // 2, g % 2
    y, xh, core = s // 4, (s // 2) % 2, s % 2

    def along_grid(r):
        return ((g + r) % GRID, s)

    def beside(dg, ds):
        return ((g + dg + 16) % 16, (s + ds + 16) % 16)

    def chip(dy, cross, dc):
        xh2 = (xh + cross) % 2
        xl2 = (xl + cross) % 2
        return (z * 2 + xl2, (((y + dy) % 4) * 2 + xh2) * 2 + (core + dc) % 2)

    sibling = chip(0, 0, 1)
    partners = [along_grid(r) for r in range(1, GRID)]
    partners += [beside(*o) for o in HALO]
    partners += [chip(*o) for o in FAR]
    partners += [sibling]
    barrier = pltpu.get_barrier_semaphore()
    for partner in partners:
        pl.semaphore_signal(barrier, inc=1, device_id=partner, device_id_type=MESH)

    cellsrc[...] = jnp.broadcast_to(cell_ref[...], (8, 128))
    lane = lax.broadcasted_iota(jnp.int32, (128, 128), 1)
    packed = jnp.zeros((128, 128), F32)
    for a, ref in enumerate((u_ref, up_ref, b_ref, m_ref)):
        rowsrc[0, a] = ref[0:8, :]
        rowsrc[1, a] = ref[120:128, :]
        both = jnp.where(lane < 64, ref[:, 0:128], ref[:, 128:256])
        packed = jnp.where(lane // 8 == a, pltpu.roll(both, 8 * a + 4, 1), packed)
    colsrc[...] = jnp.transpose(packed)[0:32].reshape(4, 8, 128)
    wide = spectra_ref[...].astype(F32)
    phased[0] = (wide * cos_ref[...]).astype(BF16)
    phased[1] = (wide * sin_ref[...]).astype(BF16)
    for slot, (dy, cross) in enumerate(SLOTS):
        source = ((y + dy) % 4) * 2 + (xh + cross) % 2
        columns = pl.ds(pl.multiple_of(source * SUBCHIP, SUBCHIP), SUBCHIP)
        classown[:, slot * SUBCHIP : (slot + 1) * SUBCHIP] = (
            class_ref[:, columns].astype(F32).astype(BF16)
        )

    pl.semaphore_wait(barrier, len(partners))

    def remote(src, dst, send, recv, target):
        return pltpu.make_async_remote_copy(
            src_ref=src, dst_ref=dst, send_sem=send, recv_sem=recv, device_id=target, device_id_type=MESH
        )

    halo_copies = []
    for i, (dg, ds) in enumerate(HALO):
        if ds == 0:
            side = 1 if dg == 1 else 0
            src, dst = rowsrc.at[side], rowin.at[side]
        elif dg == 0:
            src, dst = colsrc, colin.at[1 if ds == 1 else 0]
        else:
            side = 1 if dg == 1 else 0
            half = 1 if ds == 1 else 0
            src = rowsrc.at[side, :, :, pl.ds(half * 128, 128)]
            dst = cornerin.at[side * 2 + half]
        halo_copies.append(remote(src, dst, halo_send.at[i], halo_recv.at[i], beside(dg, ds)))
    cell_copies = [
        remote(cellsrc, cells.at[GRID - r], cell_send.at[r], cell_recv.at[r], along_grid(r)) for r in range(1, GRID)
    ]
    far_copies = []
    for i, (dy, cross, dc) in enumerate(FAR):
        slot = SLOTS.index(((4 - dy) % 4, cross))
        far_copies.append(
            remote(
                phased.at[(core + dc) % 2],
                pieces.at[slot, pl.ds(pl.multiple_of(core * 128, 128), 128)],
                far_send.at[i],
                far_recv.at[i],
                chip(dy, cross, dc),
            )
        )
    sib_piece = remote(
        phased.at[1 - core],
        pieces.at[0, pl.ds(pl.multiple_of(core * 128, 128), 128)],
        sib_send.at[0],
        sib_recv.at[0],
        sibling,
    )
    sib_class = remote(classown, classsib, sib_send.at[1], sib_recv.at[1], sibling)
    for copy in halo_copies + cell_copies + [sib_class, sib_piece] + far_copies:
        copy.start()

    pieces[0, pl.ds(pl.multiple_of(core * 128, 128), 128)] = phased[core]
    cells[0] = cellsrc[...]

    def expand(which, classes):
        held = classes[...]
        for c in range(1, CLASSES):
            onehot[which, (c - 1) * 128 : c * 128, :] = jnp.where(held == BF16(c), BF16(1), BF16(0))
        onehot[which, 896:912, :] = jnp.ones((16, 2048), BF16)

    expand(0, classown)

    for copy in halo_copies:
        copy.wait_recv()
    zero = F32(0)
    lane8 = lax.broadcasted_iota(jnp.int32, (8, 128), 1)
    sub8 = lax.broadcasted_iota(jnp.int32, (8, 128), 0)
    sub8w = lax.broadcasted_iota(jnp.int32, (8, 256), 0)
    below, above = g < 15, g > 0
    right, left = s < 15, s > 0
    sides = []
    for a in range(4):
        sides.append(
            jnp.where(sub8 < 4, jnp.where(left, colin[1, a], zero), jnp.where(right, colin[0, a], zero))
        )
    columns = jnp.transpose(jnp.concatenate(sides + [jnp.zeros((96, 128), F32)], axis=0))
    for a, ref in enumerate((u_ref, up_ref, b_ref, m_ref)):
        ext[a, 0:128, 0:256] = ref[...]
        ext[a, 0:128, 256:384] = pltpu.roll(columns, 128 - (8 * a + 4), 1)
        ext[a, 128:136, 0:256] = jnp.where(
            sub8w < 4, jnp.where(below, rowin[0, a], zero), jnp.where(above, rowin[1, a], zero)
        )
        ext[a, 128:136, 256:384] = jnp.where(
            sub8 < 4,
            jnp.where(
                lane8 < 64,
                jnp.where(below & right, cornerin[0, a], zero),
                jnp.where(below & left, cornerin[1, a], zero),
            ),
            jnp.where(
                lane8 < 64,
                jnp.where(above & right, cornerin[2, a], zero),
                jnp.where(above & left, cornerin[3, a], zero),
            ),
        )
    current, previous, buoyancy, modulus = ext[0], ext[1], ext[2], ext[3]
    rows, cols = current.shape
    down = 0.5 * (modulus + pltpu.roll(modulus, rows - 1, 0))
    along = 0.5 * (modulus + pltpu.roll(modulus, cols - 1, 1))
    for step in range(STEPS):
        flux_x = down * (pltpu.roll(current, rows - 1, 0) - current)
        flux_y = along * (pltpu.roll(current, cols - 1, 1) - current)
        div = flux_x - pltpu.roll(flux_x, 1, 0) + flux_y - pltpu.roll(flux_y, 1, 1)
        following = 2.0 * current - previous + buoyancy * div
        previous, current = current, following
        block = current[0:128, 0:256]
        coarse = block.astype(BF16)
        ush[step, 0:128, :] = coarse
        ush[step, 128:256, :] = (block - coarse.astype(F32)).astype(BF16)
        if step == STEPS - 1:
            ufinal_ref[...] = block

    for copy in cell_copies:
        copy.wait_recv()
    row_at = lax.broadcasted_iota(jnp.int32, (128, 128), 0)
    col_at = lax.broadcasted_iota(jnp.int32, (256, 128), 0)
    samp_copies = [
        remote(sampsrc.at[r], sampin.at[GRID - r], samp_send.at[r], samp_recv.at[r], along_grid(r))
        for r in range(1, GRID)
    ]
    for pair in range(0, GRID, 2):
        picks, inside = [], []
        for r in (pair, pair + 1):
            cell = cells[r, 0:1, :]
            row = lax.shift_right_logical(cell, 12) - g * 128
            col = lax.bitwise_and(cell, 4095) - s * 256
            picks.append(jnp.where(col_at == col, F32(1), zero).astype(BF16))
            inside.append(row_at == row)
        found = jnp.dot(
            ush[...].reshape(4 * 256, 256), jnp.concatenate(picks, axis=1), preferred_element_type=F32
        )
        mask = jnp.concatenate(inside, axis=1)
        recorded = []
        for step in range(STEPS):
            both = found[step * 256 : step * 256 + 128] + found[step * 256 + 128 : step * 256 + 256]
            recorded.append(jnp.sum(jnp.where(mask, both, zero), axis=0, keepdims=True))
        recorded = jnp.concatenate(recorded + [jnp.zeros((4, 256), F32)], axis=0)
        sampsrc[pair] = recorded[:, 0:128]
        sampsrc[pair + 1] = recorded[:, 128:256]
        for r in (pair, pair + 1):
            if r > 0:
                samp_copies[r - 1].start()

    sib_class.wait_recv()
    expand(1, classsib)

    for slot in range(8):
        if slot == 0:
            sib_piece.wait_recv()
        else:
            dy, cross = SLOTS[slot]
            for dc in (0, 1):
                far_copies[FAR.index(((4 - dy) % 4, cross, dc))].wait_recv()
        for n in (0, 256):
            part = pl.ds(slot * SUBCHIP, SUBCHIP)
            weights = pieces[slot, :, n : n + 256]
            first = filter_ref[0:1, n : n + 256]
            total = jnp.dot(onehot[0, 896:912, part], weights, preferred_element_type=F32)
            acc = first * total[0:1]
            for c in range(1, CLASSES):
                lhs = onehot[:, (c - 1) * 128 : c * 128, part].reshape(256, SUBCHIP)
                acc = acc + (filter_ref[c : c + 1, n : n + 256] - first) * jnp.dot(
                    lhs, weights, preferred_element_type=F32
                )
            acc = acc.reshape(2, 128, 256)
            if slot == 0:
                high[:, :, n : n + 256] = acc
            else:
                high[:, :, n : n + 256] += acc

    sib_high = remote(high.at[1], highin, sib_send.at[2], sib_recv.at[2], sibling)
    sib_high.start()

    for copy in samp_copies:
        copy.wait_recv()
    samples = sampsrc[0]
    for r in range(1, GRID):
        samples = samples + sampin[r]
    across = jnp.transpose(jnp.concatenate([samples, jnp.zeros((120, 128), F32)], axis=0))
    basis = basis_ref[...]
    low = across[:, 0:1] * basis[0:1, :]
    for step in range(1, STEPS):
        low = low + across[:, step : step + 1] * basis[step : step + 1, :]
    lowpass = jnp.concatenate([cross_ref[...], cross_ref[...]], axis=1)
    weight = lowpass * (1.0 - lowpass)
    numer = jnp.sum(weight * low * low, axis=1, keepdims=True) * (1.0 / 1024)
    sib_high.wait_recv()
    mine, other = high[0], highin[...]
    full = jnp.concatenate(
        [jnp.where(core == 0, mine, other), jnp.where(core == 0, other, mine)], axis=1
    )
    denom = jnp.sum(weight * full * full, axis=1, keepdims=True) * (1.0 / 1024)
    ratio = jnp.sqrt((numer + 1e-06) / (denom + 1e-06))
    out_ref[...] = lowpass * low + (1.0 - lowpass) * (ratio * full)

    for copy in halo_copies + cell_copies + samp_copies + far_copies + [sib_piece, sib_class, sib_high]:
        copy.wait_send()


def local(
    u_now,
    u_prev,
    buoyancy,
    modulus,
    station_cell,
    path_class,
    spectra,
    cos_table,
    sin_table,
    path_filter,
    lf_basis,
    crossover,
):
    vmem = pl.BlockSpec(memory_space=pltpu.VMEM)
    dma = pltpu.SemaphoreType.DMA
    return tuple(
        pl.pallas_call(
            kernel,
            out_shape=(
                jax.ShapeDtypeStruct((128, 1024), F32),
                jax.ShapeDtypeStruct((128, 256), F32),
            ),
            in_specs=[vmem] * 12,
            out_specs=(vmem, vmem),
            scratch_shapes=[
                pltpu.VMEM((16, 8, 128), jnp.int32),
                pltpu.VMEM((8, 128), jnp.int32),
                pltpu.VMEM((2, 4, 8, 256), F32),
                pltpu.VMEM((4, 8, 128), F32),
                pltpu.VMEM((2, 4, 8, 256), F32),
                pltpu.VMEM((2, 4, 8, 128), F32),
                pltpu.VMEM((4, 4, 8, 128), F32),
                pltpu.VMEM((4, 136, 384), F32),
                pltpu.VMEM((4, 256, 256), BF16),
                pltpu.VMEM((16, 8, 128), F32),
                pltpu.VMEM((16, 8, 128), F32),
                pltpu.VMEM((128, 2048), BF16),
                pltpu.VMEM((128, 2048), BF16),
                pltpu.VMEM((2, 912, 2048), BF16),
                pltpu.VMEM((2, 128, 512), BF16),
                pltpu.VMEM((8, 256, 512), BF16),
                pltpu.VMEM((2, 128, 512), F32),
                pltpu.VMEM((128, 512), F32),
                dma((16,)),
                dma((16,)),
                dma((8,)),
                dma((8,)),
                dma((16,)),
                dma((16,)),
                dma((14,)),
                dma((14,)),
                dma((3,)),
                dma((3,)),
            ],
            compiler_params=pltpu.CompilerParams(
                collective_id=0, has_side_effects=True, vmem_limit_bytes=48 * 1024 * 1024
            ),
        )(
            u_now,
            u_prev,
            buoyancy,
            modulus,
            station_cell.reshape(1, 128),
            path_class,
            spectra,
            cos_table,
            sin_table,
            path_filter,
            lf_basis,
            crossover.reshape(1, 512),
        )
    )


def solution(mesh):
    in_specs = (
        P("grid", "sta"),
        P("grid", "sta"),
        P("grid", "sta"),
        P("grid", "sta"),
        P(("grid", "sta")),
        P(("grid", "sta"), None),
        P("sta", None),
        P("sta", None),
        P("sta", None),
        P(),
        P(),
        P(),
    )
    out_specs = (P(("grid", "sta"), None), P("grid", "sta"))
    return jax.shard_map(local, mesh=mesh, in_specs=in_specs, out_specs=out_specs, check_vma=False)
```

time: 269 us -> 52.8 us (0.20)
  the two profiles are of different devices: /device:TPU:8 before, /device:TPU:1 now
where the time goes in v1:
time: 52.8 us; the launch traced here: 52.4 us
  Pallas kernels  40.5 us (77%)
  local copies, waits for them, and re-layouts  11.2 us (21%)
  between operations  0.67 us (1%)
    pallas_call x1, Pallas kernels, local(): pl.pallas_call(kernel, out_shape=(jax.ShapeDtypeStruct((128, 1024), F32),...  40.5 us
    unnamed x26, local copies, waits for them, and re-layouts  11.2 us

profile of v1, /device:TPU:1, one launch (start us, length us, event | category | flops | bytes accessed | tf_op | source)
XLA Modules:
  0.0 52.4 jit_solution(5082890195049488349)
XLA Ops:
  0.6 0.0 copy-start.10
  0.6 0.0 copy-start.11
  0.7 0.7 %copy-done.10 = f32[512]{0:T(512)S(1)} copy-done((f32[512]{0:T(512)S(1)}, f32[512]{0:T(512)}, u32[]{:S(2)}) %copy-start.10) | copy-done | bytes 2072
  1.3 0.0 copy-done.11
  1.3 0.0 copy-start
  1.3 1.2 %copy-done = s32[128,2048]{1,0:T(8,128)S(1)} copy-done((s32[128,2048]{1,0:T(8,128)S(1)}, s32[128,2048]{1,0:T(8,128)}, u32[]{:S(2)}) %copy-start) | copy-done | bytes 1048600
  2.5 0.0 copy-start.1
  2.5 0.9 %copy-done.1 = f32[128,512]{1,0:T(8,128)S(1)} copy-done((f32[128,512]{1,0:T(8,128)S(1)}, f32[128,512]{1,0:T(8,128)}, u32[]{:S(2)}) %copy-start.1) | copy-done | bytes 262168
  3.5 0.0 copy-start.2
  3.5 0.9 %copy-done.2 = f32[128,512]{1,0:T(8,128)S(1)} copy-done((f32[128,512]{1,0:T(8,128)S(1)}, f32[128,512]{1,0:T(8,128)}, u32[]{:S(2)}) %copy-start.2) | copy-done | bytes 262168
  4.4 0.0 copy-start.3
  4.4 0.9 %copy-done.3 = f32[128,256]{1,0:T(8,128)S(1)} copy-done((f32[128,256]{1,0:T(8,128)S(1)}, f32[128,256]{1,0:T(8,128)}, u32[]{:S(2)}) %copy-start.3) | copy-done | bytes 131096
  5.4 0.0 copy-start.4
  5.4 0.9 %copy-done.4 = f32[128,256]{1,0:T(8,128)S(1)} copy-done((f32[128,256]{1,0:T(8,128)S(1)}, f32[128,256]{1,0:T(8,128)}, u32[]{:S(2)}) %copy-start.4) | copy-done | bytes 131096
  6.3 0.0 copy-start.5
  6.3 0.9 %copy-done.5 = f32[128,256]{1,0:T(8,128)S(1)} copy-done((f32[128,256]{1,0:T(8,128)S(1)}, f32[128,256]{1,0:T(8,128)}, u32[]{:S(2)}) %copy-start.5) | copy-done | bytes 131096
  7.2 0.0 copy-start.6
  7.2 0.9 %copy-done.6 = f32[128,256]{1,0:T(8,128)S(1)} copy-done((f32[128,256]{1,0:T(8,128)S(1)}, f32[128,256]{1,0:T(8,128)}, u32[]{:S(2)}) %copy-start.6) | copy-done | bytes 131096
  8.1 0.0 copy-start.7
  8.1 0.9 %copy-done.7 = bf16[128,512]{1,0:T(8,128)(2,1)S(1)} copy-done((bf16[128,512]{1,0:T(8,128)(2,1)S(1)}, bf16[128,512]{1,0:T(8,128)(2,1)}, u32[]{:S(2)}) %copy-start.7) | copy-done | bytes 131096
  9.0 0.0 copy-start.8
  9.0 0.7 %copy-done.8 = f32[8,512]{1,0:T(8,128)S(1)} copy-done((f32[8,512]{1,0:T(8,128)S(1)}, f32[8,512]{1,0:T(8,128)}, u32[]{:S(2)}) %copy-start.8) | copy-done | bytes 16408
  9.7 0.0 copy-start.9
  9.7 0.7 %copy-done.9 = f32[4,1024]{1,0:T(4,128)S(1)} copy-done((f32[4,1024]{1,0:T(4,128)S(1)}, f32[4,1024]{1,0:T(4,128)}, u32[]{:S(2)}) %copy-start.9) | copy-done | bytes 16408
  10.4 40.5 %shard_map.131 = (f32[128,1024]{1,0:T(8,128)S(1)}, f32[128,256]{1,0:T(8,128)S(1)}) custom-call(f32[128,256]{1,0:T(8,128)S(1)} %copy-done.3, f32[128,256]{1,0:T(8,128)S(1)} %copy-done.4, f32[128,256]{1,0:T(8,128)S(1)} %copy-done.5, f32[128,256]{1,0:T(8,128)S(1)} %copy-done.6, s32[1,128]{1,0:T(1,128)S(1)} %bitcast.3, s32[128,2048]{1,0:T(8,128)S(1)} %copy-done, ...), custom_call_target="tpu_custom_call" | custom-call | tf_op jit(solution)/shard_map/pallas_call | solution.py:322
  50.9 0.8 %copy.16 = f32[128,1024]{1,0:T(8,128)} copy(f32[128,1024]{1,0:T(8,128)S(1)} %get-tuple-element.4) | data formatting | bytes 1048576
  51.7 0.7 %copy.17 = f32[128,256]{1,0:T(8,128)} copy(f32[128,256]{1,0:T(8,128)S(1)} %get-tuple-element.5) | data formatting | bytes 262144
Async XLA Ops:
  0.6 0.7 %copy-start.10 = (f32[512]{0:T(512)S(1)}, f32[512]{0:T(512)}, u32[]{:S(2)}) copy-start(f32[512]{0:T(512)} %param.23) | copy-start | bytes 6148
  0.6 0.7 %copy-start.11 = (s32[128]{0:T(128)S(1)}, s32[128]{0:T(128)}, u32[]{:S(2)}) copy-start(s32[128]{0:T(128)} %param.16) | copy-start | bytes 1540
  1.3 1.2 %copy-start = (s32[128,2048]{1,0:T(8,128)S(1)}, s32[128,2048]{1,0:T(8,128)}, u32[]{:S(2)}) copy-start(s32[128,2048]{1,0:T(8,128)} %class_ref.1) | copy-start | bytes 3145732
  2.5 0.9 %copy-start.1 = (f32[128,512]{1,0:T(8,128)S(1)}, f32[128,512]{1,0:T(8,128)}, u32[]{:S(2)}) copy-start(f32[128,512]{1,0:T(8,128)} %cos_ref.1) | copy-start | bytes 786436
  3.5 0.9 %copy-start.2 = (f32[128,512]{1,0:T(8,128)S(1)}, f32[128,512]{1,0:T(8,128)}, u32[]{:S(2)}) copy-start(f32[128,512]{1,0:T(8,128)} %sin_ref.1) | copy-start | bytes 786436
  4.4 0.9 %copy-start.3 = (f32[128,256]{1,0:T(8,128)S(1)}, f32[128,256]{1,0:T(8,128)}, u32[]{:S(2)}) copy-start(f32[128,256]{1,0:T(8,128)} %u_ref.1) | copy-start | bytes 393220
  5.4 0.9 %copy-start.4 = (f32[128,256]{1,0:T(8,128)S(1)}, f32[128,256]{1,0:T(8,128)}, u32[]{:S(2)}) copy-start(f32[128,256]{1,0:T(8,128)} %up_ref.1) | copy-start | bytes 393220
  6.3 0.9 %copy-start.5 = (f32[128,256]{1,0:T(8,128)S(1)}, f32[128,256]{1,0:T(8,128)}, u32[]{:S(2)}) copy-start(f32[128,256]{1,0:T(8,128)} %b_ref.1) | copy-start | bytes 393220
  7.2 0.9 %copy-start.6 = (f32[128,256]{1,0:T(8,128)S(1)}, f32[128,256]{1,0:T(8,128)}, u32[]{:S(2)}) copy-start(f32[128,256]{1,0:T(8,128)} %m_ref.1) | copy-start | bytes 393220
  8.1 0.9 %copy-start.7 = (bf16[128,512]{1,0:T(8,128)(2,1)S(1)}, bf16[128,512]{1,0:T(8,128)(2,1)}, u32[]{:S(2)}) copy-start(bf16[128,512]{1,0:T(8,128)(2,1)} %spectra_ref.1) | copy-start | bytes 393220
  9.0 0.7 %copy-start.8 = (f32[8,512]{1,0:T(8,128)S(1)}, f32[8,512]{1,0:T(8,128)}, u32[]{:S(2)}) copy-start(f32[8,512]{1,0:T(8,128)} %filter_ref.1) | copy-start | bytes 49156
  9.7 0.7 %copy-start.9 = (f32[4,1024]{1,0:T(4,128)S(1)}, f32[4,1024]{1,0:T(4,128)}, u32[]{:S(2)}) copy-start(f32[4,1024]{1,0:T(4,128)} %basis_ref.1) | copy-start | bytes 49156

commit v2 on v1

--- a/solution.py
+++ b/solution.py
@@ -14,8 +14,18 @@
 F32 = jnp.float32
 
 SLOTS = ((0, 0), (0, 1), (1, 0), (3, 0), (1, 1), (3, 1), (2, 0), (2, 1))
-FAR = [(dy, cross, dc) for dy, cross in SLOTS[1:] for dc in (0, 1)]
-HALO = [(-1, 0), (1, 0), (0, -1), (0, 1), (-1, -1), (-1, 1), (1, -1), (1, 1)]
+CUTS = (
+    None,
+    (0, 32, 48, 64),
+    (0, 16, 48, 64),
+    (0, 16, 32, 64),
+    (0, 32, 48, 64),
+    (0, 16, 48, 64),
+    (0, 32, 48, 64),
+    (0, 16, 32, 64),
+)
+SIDES = [(0, -1), (0, 1), (-1, -1), (-1, 1), (1, -1), (1, 1)]
+HALO = [(-1, 0), (1, 0)] + SIDES
 GRID = 16
 SUBCHIP = 256
 
@@ -35,9 +45,16 @@
     cross_ref,
     out_ref,
     ufinal_ref,
+    cellraw,
+    classraw,
+    spectra,
+    cosines,
+    sines,
+    filters,
+    bases,
+    crossing,
     cells,
     cellsrc,
-    rowsrc,
     colsrc,
     rowin,
     colin,
@@ -53,14 +70,19 @@
     pieces,
     high,
     highin,
+    load_sem,
     cell_send,
     cell_recv,
     halo_send,
     halo_recv,
     samp_send,
     samp_recv,
-    far_send,
-    far_recv,
+    near_send,
+    near_recv,
+    relay_send,
+    relay_recv,
+    plane_send,
+    plane_recv,
     sib_send,
     sib_recv,
 ):
@@ -68,6 +90,7 @@
     s = lax.axis_index("sta")
     z, xl = g // 2, g % 2
     y, xh, core = s // 4, (s // 2) % 2, s % 2
+    colour = (z + xl) % 2
 
     def along_grid(r):
         return ((g + r) % GRID, s)
@@ -81,80 +104,112 @@
         return (z * 2 + xl2, (((y + dy) % 4) * 2 + xh2) * 2 + (core + dc) % 2)
 
     sibling = chip(0, 0, 1)
-    partners = [along_grid(r) for r in range(1, GRID)]
-    partners += [beside(*o) for o in HALO]
-    partners += [chip(*o) for o in FAR]
-    partners += [sibling]
+    plane = [((g + 2) % 16, s), ((g + 14) % 16, s), (z * 2 + 1 - xl, s)]
+    near = [(dy, cross, dc) for dy, cross in ((1, 0), (3, 0), (0, 1)) for dc in (0, 1)]
+    partners = [chip(*o) for o in near] + [sibling]
+    partners += [beside(*o) for o in SIDES]
+    partners += [along_grid(r) for r in range(1, GRID)]
     barrier = pltpu.get_barrier_semaphore()
     for partner in partners:
         pl.semaphore_signal(barrier, inc=1, device_id=partner, device_id_type=MESH)
 
-    cellsrc[...] = jnp.broadcast_to(cell_ref[...], (8, 128))
+    def load(i, src, dst):
+        copy = pltpu.make_async_copy(src, dst, load_sem.at[i])
+        copy.start()
+        return copy
+
+    load_cell = load(0, cell_ref, cellraw)
+    load_grid = [
+        load(1 + a, ref, ext.at[a, pl.ds(0, 128), pl.ds(0, 256)])
+        for a, ref in enumerate((u_ref, up_ref, b_ref, m_ref))
+    ]
+    load_phase = [load(5, spectra_ref, spectra), load(6, cos_ref, cosines), load(7, sin_ref, sines)]
+    load_class = load(8, class_ref, classraw)
+    load_rest = [load(9, filter_ref, filters), load(10, basis_ref, bases), load(11, cross_ref, crossing)]
+
+    load_cell.wait()
+    cellsrc[...] = jnp.broadcast_to(cellraw[...], (8, 128))
     lane = lax.broadcasted_iota(jnp.int32, (128, 128), 1)
     packed = jnp.zeros((128, 128), F32)
-    for a, ref in enumerate((u_ref, up_ref, b_ref, m_ref)):
-        rowsrc[0, a] = ref[0:8, :]
-        rowsrc[1, a] = ref[120:128, :]
-        both = jnp.where(lane < 64, ref[:, 0:128], ref[:, 128:256])
+    for a in range(4):
+        load_grid[a].wait()
+        both = jnp.where(lane < 64, ext[a, 0:128, 0:128], ext[a, 0:128, 128:256])
         packed = jnp.where(lane // 8 == a, pltpu.roll(both, 8 * a + 4, 1), packed)
     colsrc[...] = jnp.transpose(packed)[0:32].reshape(4, 8, 128)
-    wide = spectra_ref[...].astype(F32)
-    phased[0] = (wide * cos_ref[...]).astype(BF16)
-    phased[1] = (wide * sin_ref[...]).astype(BF16)
+    for copy in load_phase:
+        copy.wait()
+    wide = spectra[...].astype(F32)
+    phased[0] = (wide * cosines[...]).astype(BF16).reshape(2, 64, 512)
+    phased[1] = (wide * sines[...]).astype(BF16).reshape(2, 64, 512)
+    load_class.wait()
     for slot, (dy, cross) in enumerate(SLOTS):
         source = ((y + dy) % 4) * 2 + (xh + cross) % 2
         columns = pl.ds(pl.multiple_of(source * SUBCHIP, SUBCHIP), SUBCHIP)
-        classown[:, slot * SUBCHIP : (slot + 1) * SUBCHIP] = (
-            class_ref[:, columns].astype(F32).astype(BF16)
-        )
+        classown[:, slot * SUBCHIP : (slot + 1) * SUBCHIP] = classraw[:, columns].astype(F32).astype(BF16)
 
     pl.semaphore_wait(barrier, len(partners))
 
     def remote(src, dst, send, recv, target):
-        return pltpu.make_async_remote_copy(
+        copy = pltpu.make_async_remote_copy(
             src_ref=src, dst_ref=dst, send_sem=send, recv_sem=recv, device_id=target, device_id_type=MESH
         )
+        copy.start()
+        return copy
 
     halo_copies = []
     for i, (dg, ds) in enumerate(HALO):
+        side = 1 if dg == 1 else 0
+        rows = pl.ds(120 * side, 8)
         if ds == 0:
-            side = 1 if dg == 1 else 0
-            src, dst = rowsrc.at[side], rowin.at[side]
+            src, dst = ext.at[:, rows, pl.ds(0, 256)], rowin.at[side]
         elif dg == 0:
             src, dst = colsrc, colin.at[1 if ds == 1 else 0]
         else:
-            side = 1 if dg == 1 else 0
             half = 1 if ds == 1 else 0
-            src = rowsrc.at[side, :, :, pl.ds(half * 128, 128)]
-            dst = cornerin.at[side * 2 + half]
+            src, dst = ext.at[:, rows, pl.ds(half * 128, 128)], cornerin.at[side * 2 + half]
         halo_copies.append(remote(src, dst, halo_send.at[i], halo_recv.at[i], beside(dg, ds)))
     cell_copies = [
         remote(cellsrc, cells.at[GRID - r], cell_send.at[r], cell_recv.at[r], along_grid(r)) for r in range(1, GRID)
     ]
-    far_copies = []
-    for i, (dy, cross, dc) in enumerate(FAR):
+    near_copies = []
+    for i, (dy, cross, dc) in enumerate(near):
         slot = SLOTS.index(((4 - dy) % 4, cross))
-        far_copies.append(
+        half = 1 - colour if cross else colour
+        near_copies.append(
             remote(
-                phased.at[(core + dc) % 2],
-                pieces.at[slot, pl.ds(pl.multiple_of(core * 128, 128), 128)],
-                far_send.at[i],
-                far_recv.at[i],
+                phased.at[(core + dc) % 2, half],
+                pieces.at[slot, core, half],
+                near_send.at[i],
+                near_recv.at[i],
                 chip(dy, cross, dc),
             )
         )
-    sib_piece = remote(
-        phased.at[1 - core],
-        pieces.at[0, pl.ds(pl.multiple_of(core * 128, 128), 128)],
-        sib_send.at[0],
-        sib_recv.at[0],
-        sibling,
-    )
     sib_class = remote(classown, classsib, sib_send.at[1], sib_recv.at[1], sibling)
-    for copy in halo_copies + cell_copies + [sib_class, sib_piece] + far_copies:
-        copy.start()
-
-    pieces[0, pl.ds(pl.multiple_of(core * 128, 128), 128)] = phased[core]
+    sib_piece = remote(phased.at[1 - core], pieces.at[0, core], sib_send.at[0], sib_recv.at[0], sibling)
+
+    relay_copies = []
+
+    def relay(source, dy, slot, start, size):
+        i = len(relay_copies)
+        relay_copies.append(
+            remote(
+                pieces.at[source, :, colour, pl.ds(start, size)],
+                pieces.at[slot, :, colour, pl.ds(start, size)],
+                relay_send.at[i],
+                relay_recv.at[i],
+                chip(dy, 0, 0),
+            )
+        )
+
+    plane_copies = {}
+
+    def share(slot, part):
+        start, stop = CUTS[slot][part], CUTS[slot][part + 1]
+        rows = pieces.at[slot, :, colour, pl.ds(start, stop - start)]
+        i = (slot - 1) * 3 + part
+        plane_copies[slot, part] = remote(rows, rows, plane_send.at[i], plane_recv.at[i], plane[part])
+
+    pieces[0, core] = phased[core]
     cells[0] = cellsrc[...]
 
     def expand(which, classes):
@@ -179,8 +234,7 @@
             jnp.where(sub8 < 4, jnp.where(left, colin[1, a], zero), jnp.where(right, colin[0, a], zero))
         )
     columns = jnp.transpose(jnp.concatenate(sides + [jnp.zeros((96, 128), F32)], axis=0))
-    for a, ref in enumerate((u_ref, up_ref, b_ref, m_ref)):
-        ext[a, 0:128, 0:256] = ref[...]
+    for a in range(4):
         ext[a, 0:128, 256:384] = pltpu.roll(columns, 128 - (8 * a + 4), 1)
         ext[a, 128:136, 0:256] = jnp.where(
             sub8w < 4, jnp.where(below, rowin[0, a], zero), jnp.where(above, rowin[1, a], zero)
@@ -215,14 +269,21 @@
         if step == STEPS - 1:
             ufinal_ref[...] = block
 
+    for copy in near_copies:
+        copy.wait_recv()
+    relay(1, 1, 5, 0, 64)
+    relay(1, 3, 4, 0, 64)
+    relay(3, 1, 6, 0, 32)
+    relay(2, 3, 6, 32, 32)
+    for slot in (1, 2, 3):
+        for part in range(3):
+            share(slot, part)
+
     for copy in cell_copies:
         copy.wait_recv()
     row_at = lax.broadcasted_iota(jnp.int32, (128, 128), 0)
     col_at = lax.broadcasted_iota(jnp.int32, (256, 128), 0)
-    samp_copies = [
-        remote(sampsrc.at[r], sampin.at[GRID - r], samp_send.at[r], samp_recv.at[r], along_grid(r))
-        for r in range(1, GRID)
-    ]
+    samp_copies = []
     for pair in range(0, GRID, 2):
         picks, inside = [], []
         for r in (pair, pair + 1):
@@ -244,27 +305,27 @@
         sampsrc[pair + 1] = recorded[:, 128:256]
         for r in (pair, pair + 1):
             if r > 0:
-                samp_copies[r - 1].start()
+                samp_copies.append(
+                    remote(sampsrc.at[r], sampin.at[GRID - r], samp_send.at[r], samp_recv.at[r], along_grid(r))
+                )
 
     sib_class.wait_recv()
     expand(1, classsib)
-
-    for slot in range(8):
-        if slot == 0:
-            sib_piece.wait_recv()
-        else:
-            dy, cross = SLOTS[slot]
-            for dc in (0, 1):
-                far_copies[FAR.index(((4 - dy) % 4, cross, dc))].wait_recv()
+    for copy in load_rest:
+        copy.wait()
+
+    def multiply(slot):
+        for part in range(3) if slot else ():
+            plane_copies[slot, part].wait_recv()
+        part = pl.ds(slot * SUBCHIP, SUBCHIP)
         for n in (0, 256):
-            part = pl.ds(slot * SUBCHIP, SUBCHIP)
-            weights = pieces[slot, :, n : n + 256]
-            first = filter_ref[0:1, n : n + 256]
+            weights = pieces[slot, :, :, :, n : n + 256].reshape(SUBCHIP, 256)
+            first = filters[0:1, n : n + 256]
             total = jnp.dot(onehot[0, 896:912, part], weights, preferred_element_type=F32)
             acc = first * total[0:1]
             for c in range(1, CLASSES):
                 lhs = onehot[:, (c - 1) * 128 : c * 128, part].reshape(256, SUBCHIP)
-                acc = acc + (filter_ref[c : c + 1, n : n + 256] - first) * jnp.dot(
+                acc = acc + (filters[c : c + 1, n : n + 256] - first) * jnp.dot(
                     lhs, weights, preferred_element_type=F32
                 )
             acc = acc.reshape(2, 128, 256)
@@ -273,8 +334,26 @@
             else:
                 high[:, :, n : n + 256] += acc
 
+    sib_piece.wait_recv()
+    multiply(0)
+    multiply(1)
+    for copy in relay_copies[0:4]:
+        copy.wait_recv()
+    relay(5, 1, 7, 0, 32)
+    relay(4, 3, 7, 32, 32)
+    for slot in (4, 5, 6):
+        for part in range(3):
+            share(slot, part)
+    multiply(2)
+    multiply(3)
+    for copy in relay_copies[4:6]:
+        copy.wait_recv()
+    for part in range(3):
+        share(7, part)
+    for slot in (4, 5, 6, 7):
+        multiply(slot)
+
     sib_high = remote(high.at[1], highin, sib_send.at[2], sib_recv.at[2], sibling)
-    sib_high.start()
 
     for copy in samp_copies:
         copy.wait_recv()
@@ -282,11 +361,11 @@
     for r in range(1, GRID):
         samples = samples + sampin[r]
     across = jnp.transpose(jnp.concatenate([samples, jnp.zeros((120, 128), F32)], axis=0))
-    basis = basis_ref[...]
+    basis = bases[...]
     low = across[:, 0:1] * basis[0:1, :]
     for step in range(1, STEPS):
         low = low + across[:, step : step + 1] * basis[step : step + 1, :]
-    lowpass = jnp.concatenate([cross_ref[...], cross_ref[...]], axis=1)
+    lowpass = jnp.concatenate([crossing[...], crossing[...]], axis=1)
     weight = lowpass * (1.0 - lowpass)
     numer = jnp.sum(weight * low * low, axis=1, keepdims=True) * (1.0 / 1024)
     sib_high.wait_recv()
@@ -298,7 +377,8 @@
     ratio = jnp.sqrt((numer + 1e-06) / (denom + 1e-06))
     out_ref[...] = lowpass * low + (1.0 - lowpass) * (ratio * full)
 
-    for copy in halo_copies + cell_copies + samp_copies + far_copies + [sib_piece, sib_class, sib_high]:
+    sent = halo_copies + cell_copies + samp_copies + near_copies + relay_copies + list(plane_copies.values())
+    for copy in sent + [sib_piece, sib_class, sib_high]:
         copy.wait_send()
 
 
@@ -325,12 +405,19 @@
                 jax.ShapeDtypeStruct((128, 1024), F32),
                 jax.ShapeDtypeStruct((128, 256), F32),
             ),
-            in_specs=[vmem] * 12,
+            in_specs=[pl.BlockSpec(memory_space=pl.ANY)] * 12,
             out_specs=(vmem, vmem),
             scratch_shapes=[
+                pltpu.VMEM((1, 128), jnp.int32),
+                pltpu.VMEM((128, 2048), jnp.int32),
+                pltpu.VMEM((128, 512), BF16),
+                pltpu.VMEM((128, 512), F32),
+                pltpu.VMEM((128, 512), F32),
+                pltpu.VMEM((8, 512), F32),
+                pltpu.VMEM((4, 1024), F32),
+                pltpu.VMEM((1, 512), F32),
                 pltpu.VMEM((16, 8, 128), jnp.int32),
                 pltpu.VMEM((8, 128), jnp.int32),
-                pltpu.VMEM((2, 4, 8, 256), F32),
                 pltpu.VMEM((4, 8, 128), F32),
                 pltpu.VMEM((2, 4, 8, 256), F32),
                 pltpu.VMEM((2, 4, 8, 128), F32),
@@ -342,23 +429,28 @@
                 pltpu.VMEM((128, 2048), BF16),
                 pltpu.VMEM((128, 2048), BF16),
                 pltpu.VMEM((2, 912, 2048), BF16),
-                pltpu.VMEM((2, 128, 512), BF16),
-                pltpu.VMEM((8, 256, 512), BF16),
+                pltpu.VMEM((2, 2, 64, 512), BF16),
+                pltpu.VMEM((8, 2, 2, 64, 512), BF16),
                 pltpu.VMEM((2, 128, 512), F32),
                 pltpu.VMEM((128, 512), F32),
+                dma((12,)),
                 dma((16,)),
                 dma((16,)),
                 dma((8,)),
                 dma((8,)),
                 dma((16,)),
                 dma((16,)),
-                dma((14,)),
-                dma((14,)),
+                dma((6,)),
+                dma((6,)),
+                dma((6,)),
+                dma((6,)),
+                dma((21,)),
+                dma((21,)),
                 dma((3,)),
                 dma((3,)),
             ],
             compiler_params=pltpu.CompilerParams(
-                collective_id=0, has_side_effects=True, vmem_limit_bytes=48 * 1024 * 1024
+                collective_id=0, has_side_effects=True, vmem_limit_bytes=60 * 1024 * 1024
             ),
         )(
             u_now,

time: 52.8 us -> 38.3 us (0.73)
  local copies, waits for them, and re-layouts: 11.2 us -> 2.58 us
  Pallas kernels: 40.5 us -> 35 us
    unnamed x26 -> x4, local copies, waits for them, and re-layouts: 11.2 us -> 2.58 us
    pallas_call x1, Pallas kernels: 40.5 us -> 35 us  [local(): pl.pallas_call(kernel, out_shape=(jax.ShapeDtypeStruct((128, 1024), F32),...]
where the time goes in v2:
time: 38.3 us; the launch traced here: 38.2 us
  Pallas kernels  35 us (91%)
  local copies, waits for them, and re-layouts  2.58 us (7%)
  between operations  0.65 us (2%)
    pallas_call x1, Pallas kernels, local(): pl.pallas_call(kernel, out_shape=(jax.ShapeDtypeStruct((128, 1024), F32),...  35 us
    unnamed x4, local copies, waits for them, and re-layouts  2.58 us

profile of v2, /device:TPU:1, one launch (start us, length us, event | category | flops | bytes accessed | tf_op | source)
XLA Modules:
  0.0 38.2 jit_solution(815213427710336162)
XLA Ops:
  0.6 35.0 %shard_map.131 = (f32[128,1024]{1,0:T(8,128)}, f32[128,256]{1,0:T(8,128)}) custom-call(f32[128,256]{1,0:T(8,128)} %u_ref.1, f32[128,256]{1,0:T(8,128)} %up_ref.1, f32[128,256]{1,0:T(8,128)} %b_ref.1, f32[128,256]{1,0:T(8,128)} %m_ref.1, s32[1,128]{1,0:T(1,128)} %bitcast.3, s32[128,2048]{1,0:T(8,128)} %class_ref.1, bf16[128,512]{1,0:T(8,128)(2,1)} %spectra_ref.1, ...), custom_call_target="tpu_custom_call" | custom-call | tf_op jit(solution)/shard_map/pallas_call | solution.py:402
  35.6 0.0 copy-start
  35.6 1.9 %copy.16 = f32[128,1024]{1,0:T(8,128)} copy(f32[128,1024]{1,0:T(8,128)} %get-tuple-element.4) | data formatting | bytes 1048576
  37.6 0.0 copy-done
  37.6 0.7 %copy.17 = f32[128,256]{1,0:T(8,128)} copy(f32[128,256]{1,0:T(8,128)S(1)} %copy-done) | data formatting | bytes 262144
Async XLA Ops:
  35.6 1.9 %copy-start = (f32[128,256]{1,0:T(8,128)S(1)}, f32[128,256]{1,0:T(8,128)}, u32[]{:S(2)}) copy-start(f32[128,256]{1,0:T(8,128)} %get-tuple-element.5) | copy-start | bytes 393220

commit v3 on v2

v3 whole, which is shorter than its diff:
```python
import functools

import jax
import jax.numpy as jnp
from jax import lax
from jax.experimental import pallas as pl
from jax.experimental.pallas import tpu as pltpu
from jax.sharding import PartitionSpec as P

STEPS = 4
CLASSES = 8
MESH = pl.DeviceIdType.MESH
BF16 = jnp.bfloat16
F32 = jnp.float32

SLOTS = ((0, 0), (0, 1), (1, 0), (3, 0), (1, 1), (3, 1), (2, 0), (2, 1))
SIDES = [(0, -1), (0, 1), (-1, -1), (-1, 1), (1, -1), (1, 1)]
HALO = [(-1, 0), (1, 0)] + SIDES
GRID = 16
FARTHEST = (8, 9, 7, 10, 6, 11, 5, 12, 4, 13, 3, 14, 2, 15, 1, 0)
SUBCHIP = 256


def kernel(
    u_ref,
    up_ref,
    b_ref,
    m_ref,
    cell_ref,
    class_ref,
    spectra_ref,
    cos_ref,
    sin_ref,
    filter_ref,
    mine_ref,
    other_ref,
    samples_ref,
    field_ref,
    cellraw,
    classraw,
    spectra,
    cosines,
    sines,
    filters,
    final,
    total_samples,
    cells,
    cellsrc,
    colsrc,
    rowin,
    colin,
    cornerin,
    ext,
    ush,
    sampsrc,
    sampin,
    classown,
    classsib,
    onehot,
    phased,
    pieces,
    high,
    load_sem,
    cell_send,
    cell_recv,
    halo_send,
    halo_recv,
    samp_send,
    samp_recv,
    near_send,
    near_recv,
    relay_send,
    relay_recv,
    plane_send,
    plane_recv,
    sib_send,
    sib_recv,
):
    g = lax.axis_index("grid")
    s = lax.axis_index("sta")
    z, xl = g // 2, g % 2
    y, xh, core = s // 4, (s // 2) % 2, s % 2
    colour = (z + xl) % 2

    def along_grid(r):
        return ((g + r) % GRID, s)

    def beside(dg, ds):
        return ((g + dg + 16) % 16, (s + ds + 16) % 16)

    def chip(dy, cross, dc):
        xh2 = (xh + cross) % 2
        xl2 = (xl + cross) % 2
        return (z * 2 + xl2, (((y + dy) % 4) * 2 + xh2) * 2 + (core + dc) % 2)

    sibling = chip(0, 0, 1)
    plane = [((g + 2) % 16, s), ((g + 14) % 16, s), (z * 2 + 1 - xl, s)]
    near = [(dy, cross, dc) for dy, cross in ((1, 0), (3, 0), (0, 1)) for dc in (0, 1)]
    partners = [chip(*o) for o in near] + [sibling]
    partners += [beside(*o) for o in SIDES]
    partners += [along_grid(r) for r in range(1, GRID)]
    barrier = pltpu.get_barrier_semaphore()
    for partner in partners:
        pl.semaphore_signal(barrier, inc=1, device_id=partner, device_id_type=MESH)

    def load(i, src, dst):
        copy = pltpu.make_async_copy(src, dst, load_sem.at[i])
        copy.start()
        return copy

    load_cell = load(0, cell_ref, cellraw)
    load_phase = [load(5, spectra_ref, spectra), load(6, cos_ref, cosines), load(7, sin_ref, sines)]
    load_grid = [
        load(1 + a, ref, ext.at[a, pl.ds(0, 128), pl.ds(0, 256)])
        for a, ref in enumerate((u_ref, up_ref, b_ref, m_ref))
    ]
    load_class = load(8, class_ref, classraw)
    load_filter = load(9, filter_ref, filters)

    load_cell.wait()
    cellsrc[...] = jnp.broadcast_to(cellraw[...], (8, 128))
    for copy in load_phase:
        copy.wait()
    wide = spectra[...].astype(F32)
    phased[0] = (wide * cosines[...]).astype(BF16).reshape(2, 64, 512)
    phased[1] = (wide * sines[...]).astype(BF16).reshape(2, 64, 512)
    lane = lax.broadcasted_iota(jnp.int32, (128, 128), 1)
    packed = jnp.zeros((128, 128), F32)
    for a in range(4):
        load_grid[a].wait()
        both = jnp.where(lane < 64, ext[a, 0:128, 0:128], ext[a, 0:128, 128:256])
        packed = jnp.where(lane // 8 == a, pltpu.roll(both, 8 * a + 4, 1), packed)
    colsrc[...] = jnp.transpose(packed)[0:32].reshape(4, 8, 128)

    pl.semaphore_wait(barrier, len(partners))

    def remote(src, dst, send, recv, target):
        copy = pltpu.make_async_remote_copy(
            src_ref=src, dst_ref=dst, send_sem=send, recv_sem=recv, device_id=target, device_id_type=MESH
        )
        copy.start()
        return copy

    halo_copies = []
    for i, (dg, ds) in enumerate(HALO):
        side = 1 if dg == 1 else 0
        rows = pl.ds(120 * side, 8)
        if ds == 0:
            src, dst = ext.at[:, rows, pl.ds(0, 256)], rowin.at[side]
        elif dg == 0:
            src, dst = colsrc, colin.at[1 if ds == 1 else 0]
        else:
            half = 1 if ds == 1 else 0
            src, dst = ext.at[:, rows, pl.ds(half * 128, 128)], cornerin.at[side * 2 + half]
        halo_copies.append(remote(src, dst, halo_send.at[i], halo_recv.at[i], beside(dg, ds)))
    cell_copies = [
        remote(cellsrc, cells.at[GRID - r], cell_send.at[r], cell_recv.at[r], along_grid(r)) for r in FARTHEST if r
    ]
    near_copies = {}

    def send_near(turn):
        for i, (dy, cross, dc) in enumerate(near):
            slot = SLOTS.index(((4 - dy) % 4, cross))
            half = 1 - colour if cross else colour
            part = 1 - turn if dy == 3 else turn
            rows = pl.ds(32 * part, 32)
            near_copies[dy, cross, dc, part] = remote(
                phased.at[(core + dc) % 2, half, rows],
                pieces.at[slot, core, half, rows],
                near_send.at[2 * i + part],
                near_recv.at[2 * i + part],
                chip(dy, cross, dc),
            )

    send_near(0)
    sib_piece = remote(phased.at[1 - core], pieces.at[0, core], sib_send.at[0], sib_recv.at[0], sibling)

    relay_copies = {}

    def relay(source, dy, cross, slot, part):
        i = len(relay_copies)
        rows = pl.ds(32 * part, 32)
        relay_copies[slot, cross, part] = remote(
            pieces.at[source, :, colour, rows],
            pieces.at[slot, :, colour, rows],
            relay_send.at[i],
            relay_recv.at[i],
            chip(dy, cross, 0),
        )

    plane_copies = {}

    def share(slot, part, half):
        for quarter in (2 * part, 2 * part + 1):
            rows = pieces.at[slot, :, half, pl.ds(16 * quarter, 16)]
            i = (slot - 1) * 4 + quarter
            plane_copies[slot, quarter] = remote(rows, rows, plane_send.at[i], plane_recv.at[i], plane[i % 3])

    load_class.wait()
    for slot, (dy, cross) in enumerate(SLOTS):
        source = ((y + dy) % 4) * 2 + (xh + cross) % 2
        columns = pl.ds(pl.multiple_of(source * SUBCHIP, SUBCHIP), SUBCHIP)
        classown[:, slot * SUBCHIP : (slot + 1) * SUBCHIP] = classraw[:, columns].astype(F32).astype(BF16)
    sib_class = remote(classown, classsib, sib_send.at[1], sib_recv.at[1], sibling)
    pieces[0, core] = phased[core]
    cells[0] = cellsrc[...]

    def expand(which, classes):
        held = classes[...]
        for c in range(1, CLASSES):
            onehot[which, (c - 1) * 128 : c * 128, :] = jnp.where(held == BF16(c), BF16(1), BF16(0))
        onehot[which, 896:912, :] = jnp.ones((16, 2048), BF16)

    expand(0, classown)
    send_near(1)
    sib_class.wait_recv()
    expand(1, classsib)
    load_filter.wait()

    def multiply(slot):
        for quarter in range(4) if 0 < slot < 7 else ():
            plane_copies[slot, quarter].wait_recv()
        part = pl.ds(slot * SUBCHIP, SUBCHIP)
        for n in (0, 256):
            weights = pieces[slot, :, :, :, n : n + 256].reshape(SUBCHIP, 256)
            first = filters[0:1, n : n + 256]
            total = jnp.dot(onehot[0, 896:912, part], weights, preferred_element_type=F32)
            acc = first * total[0:1]
            for c in range(1, CLASSES):
                lhs = onehot[:, (c - 1) * 128 : c * 128, part].reshape(256, SUBCHIP)
                acc = acc + (filters[c : c + 1, n : n + 256] - first) * jnp.dot(
                    lhs, weights, preferred_element_type=F32
                )
            acc = acc.reshape(2, 128, 256)
            if slot == 0:
                high[:, :, n : n + 256] = acc
            else:
                high[:, :, n : n + 256] += acc

    sib_piece.wait_recv()
    multiply(0)

    for copy in halo_copies:
        copy.wait_recv()
    zero = F32(0)
    lane8 = lax.broadcasted_iota(jnp.int32, (8, 128), 1)
    sub8 = lax.broadcasted_iota(jnp.int32, (8, 128), 0)
    sub8w = lax.broadcasted_iota(jnp.int32, (8, 256), 0)
    below, above = g < 15, g > 0
    right, left = s < 15, s > 0
    sides = []
    for a in range(4):
        sides.append(
            jnp.where(sub8 < 4, jnp.where(left, colin[1, a], zero), jnp.where(right, colin[0, a], zero))
        )
    columns = jnp.transpose(jnp.concatenate(sides + [jnp.zeros((96, 128), F32)], axis=0))
    for a in range(4):
        ext[a, 0:128, 256:384] = pltpu.roll(columns, 128 - (8 * a + 4), 1)
        ext[a, 128:136, 0:256] = jnp.where(
            sub8w < 4, jnp.where(below, rowin[0, a], zero), jnp.where(above, rowin[1, a], zero)
        )
        ext[a, 128:136, 256:384] = jnp.where(
            sub8 < 4,
            jnp.where(
                lane8 < 64,
                jnp.where(below & right, cornerin[0, a], zero),
                jnp.where(below & left, cornerin[1, a], zero),
            ),
            jnp.where(
                lane8 < 64,
                jnp.where(above & right, cornerin[2, a], zero),
                jnp.where(above & left, cornerin[3, a], zero),
            ),
        )
    current, previous, buoyancy, modulus = ext[0], ext[1], ext[2], ext[3]
    rows, cols = current.shape
    down = 0.5 * (modulus + pltpu.roll(modulus, rows - 1, 0))
    along = 0.5 * (modulus + pltpu.roll(modulus, cols - 1, 1))
    for step in range(STEPS):
        flux_x = down * (pltpu.roll(current, rows - 1, 0) - current)
        flux_y = along * (pltpu.roll(current, cols - 1, 1) - current)
        div = flux_x - pltpu.roll(flux_x, 1, 0) + flux_y - pltpu.roll(flux_y, 1, 1)
        following = 2.0 * current - previous + buoyancy * div
        previous, current = current, following
        block = current[0:128, 0:256]
        coarse = block.astype(BF16)
        ush[step, 0:128, :] = coarse
        ush[step, 128:256, :] = (block - coarse.astype(F32)).astype(BF16)
        if step == STEPS - 1:
            final[...] = block

    field_out = pltpu.make_async_copy(final, field_ref, load_sem.at[13])
    field_out.start()

    def arrived(dy, cross, part):
        for dc in (0, 1):
            near_copies[dy, cross, dc, part].wait_recv()

    for copy in ((1, 0, 0), (3, 0, 1), (0, 1, 0)):
        arrived(*copy)
    relay(3, 1, 0, 6, 0)
    relay(2, 3, 0, 6, 1)
    share(3, 0, colour)
    share(2, 1, colour)
    share(1, 0, colour)
    for copy in ((1, 0, 1), (3, 0, 0), (0, 1, 1)):
        arrived(*copy)
    relay(1, 1, 0, 5, 0)
    relay(1, 3, 0, 4, 1)
    relay(3, 0, 1, 5, 1)
    relay(2, 0, 1, 4, 0)
    share(1, 1, colour)
    share(3, 1, colour)
    share(2, 0, colour)

    for copy in cell_copies:
        copy.wait_recv()
    row_at = lax.broadcasted_iota(jnp.int32, (128, 128), 0)
    col_at = lax.broadcasted_iota(jnp.int32, (256, 128), 0)
    samp_copies = []
    for pair in range(0, GRID, 2):
        pair = FARTHEST[pair : pair + 2]
        picks, inside = [], []
        for r in pair:
            cell = cells[r, 0:1, :]
            row = lax.shift_right_logical(cell, 12) - g * 128
            col = lax.bitwise_and(cell, 4095) - s * 256
            picks.append(jnp.where(col_at == col, F32(1), zero).astype(BF16))
            inside.append(row_at == row)
        found = jnp.dot(
            ush[...].reshape(4 * 256, 256), jnp.concatenate(picks, axis=1), preferred_element_type=F32
        )
        mask = jnp.concatenate(inside, axis=1)
        recorded = []
        for step in range(STEPS):
            both = found[step * 256 : step * 256 + 128] + found[step * 256 + 128 : step * 256 + 256]
            recorded.append(jnp.sum(jnp.where(mask, both, zero), axis=0, keepdims=True))
        recorded = jnp.concatenate(recorded + [jnp.zeros((4, 256), F32)], axis=0)
        sampsrc[pair[0]] = recorded[:, 0:128]
        sampsrc[pair[1]] = recorded[:, 128:256]
        for r in pair:
            if r > 0:
                samp_copies.append(
                    remote(sampsrc.at[r], sampin.at[GRID - r], samp_send.at[r], samp_recv.at[r], along_grid(r))
                )

    relay_copies[6, 0, 0].wait_recv()
    relay_copies[6, 0, 1].wait_recv()
    relay(6, 0, 1, 7, 0)
    relay(6, 0, 1, 7, 1)
    share(6, 0, colour)
    share(6, 1, colour)
    relay_copies[5, 0, 0].wait_recv()
    relay(5, 1, 0, 7, 0)
    relay_copies[4, 0, 1].wait_recv()
    relay(4, 3, 0, 7, 1)
    share(5, 0, colour)
    share(4, 1, colour)
    multiply(1)
    relay_copies[5, 1, 1].wait_recv()
    relay_copies[4, 1, 0].wait_recv()
    share(5, 1, 1 - colour)
    share(4, 0, 1 - colour)
    for slot in (2, 3, 6):
        multiply(slot)
    for cross in (0, 1):
        for part in (0, 1):
            relay_copies[7, cross, part].wait_recv()
    multiply(7)
    multiply(4)
    multiply(5)

    sib_high = remote(high.at[1], other_ref, sib_send.at[2], sib_recv.at[2], sibling)
    mine_out = pltpu.make_async_copy(high.at[0], mine_ref, load_sem.at[12])
    mine_out.start()
    for copy in samp_copies:
        copy.wait_recv()
    samples = sampsrc[0]
    for r in range(1, GRID):
        samples = samples + sampin[r]
    total_samples[...] = samples
    samples_out = pltpu.make_async_copy(total_samples, samples_ref, load_sem.at[14])
    samples_out.start()
    sib_high.wait_recv()
    mine_out.wait()
    samples_out.wait()
    field_out.wait()

    sent = halo_copies + cell_copies + samp_copies + list(near_copies.values()) + list(relay_copies.values())
    sent += list(plane_copies.values())
    for copy in sent + [sib_piece, sib_class, sib_high]:
        copy.wait_send()


def merge(
    mine_ref,
    other_ref,
    samples_ref,
    field_ref,
    basis_ref,
    cross_ref,
    out_ref,
    ufinal_ref,
    halves,
    samples,
    bases,
    crossing,
    out,
    field,
    sem,
):
    core = lax.axis_index("sta") % 2
    field_in = pltpu.make_async_copy(field_ref, field, sem.at[0])
    field_out = pltpu.make_async_copy(field, ufinal_ref, sem.at[7])
    loads = [
        pltpu.make_async_copy(samples_ref, samples, sem.at[1]),
        pltpu.make_async_copy(basis_ref, bases, sem.at[2]),
        pltpu.make_async_copy(cross_ref, crossing, sem.at[3]),
    ]
    halves_in = [
        pltpu.make_async_copy(mine_ref, halves.at[core], sem.at[4]),
        pltpu.make_async_copy(other_ref, halves.at[1 - core], sem.at[5]),
    ]
    for copy in loads:
        copy.start()
    for copy in halves_in:
        copy.start()
    field_in.start()
    for copy in loads:
        copy.wait()
    across = jnp.transpose(jnp.concatenate([samples[...], jnp.zeros((120, 128), F32)], axis=0))
    basis = bases[...]
    lowpass = jnp.concatenate([crossing[...], crossing[...]], axis=1)
    weight = lowpass * (1.0 - lowpass)
    low = across[:, 0:1] * basis[0:1, :]
    for step in range(1, STEPS):
        low = low + across[:, step : step + 1] * basis[step : step + 1, :]
    numer = jnp.sum(weight * low * low, axis=1, keepdims=True) * (1.0 / 1024)
    field_in.wait()
    field_out.start()
    for copy in halves_in:
        copy.wait()
    full = jnp.concatenate([halves[0], halves[1]], axis=1)
    denom = jnp.sum(weight * full * full, axis=1, keepdims=True) * (1.0 / 1024)
    ratio = jnp.sqrt((numer + 1e-06) / (denom + 1e-06))
    out[...] = lowpass * low + (1.0 - lowpass) * (ratio * full)
    store = pltpu.make_async_copy(out, out_ref, sem.at[6])
    store.start()
    field_out.wait()
    store.wait()


def local(
    u_now,
    u_prev,
    buoyancy,
    modulus,
    station_cell,
    path_class,
    spectra,
    cos_table,
    sin_table,
    path_filter,
    lf_basis,
    crossover,
):
    dma = pltpu.SemaphoreType.DMA
    anywhere = pl.BlockSpec(memory_space=pl.ANY)
    mine, other, samples, field = pl.pallas_call(
            kernel,
            out_shape=(
                jax.ShapeDtypeStruct((128, 512), F32),
                jax.ShapeDtypeStruct((128, 512), F32),
                jax.ShapeDtypeStruct((8, 128), F32),
                jax.ShapeDtypeStruct((128, 256), F32),
            ),
            in_specs=[anywhere] * 10,
            out_specs=(anywhere,) * 4,
            scratch_shapes=[
                pltpu.VMEM((1, 128), jnp.int32),
                pltpu.VMEM((128, 2048), jnp.int32),
                pltpu.VMEM((128, 512), BF16),
                pltpu.VMEM((128, 512), F32),
                pltpu.VMEM((128, 512), F32),
                pltpu.VMEM((8, 512), F32),
                pltpu.VMEM((128, 256), F32),
                pltpu.VMEM((8, 128), F32),
                pltpu.VMEM((16, 8, 128), jnp.int32),
                pltpu.VMEM((8, 128), jnp.int32),
                pltpu.VMEM((4, 8, 128), F32),
                pltpu.VMEM((2, 4, 8, 256), F32),
                pltpu.VMEM((2, 4, 8, 128), F32),
                pltpu.VMEM((4, 4, 8, 128), F32),
                pltpu.VMEM((4, 136, 384), F32),
                pltpu.VMEM((4, 256, 256), BF16),
                pltpu.VMEM((16, 8, 128), F32),
                pltpu.VMEM((16, 8, 128), F32),
                pltpu.VMEM((128, 2048), BF16),
                pltpu.VMEM((128, 2048), BF16),
                pltpu.VMEM((2, 912, 2048), BF16),
                pltpu.VMEM((2, 2, 64, 512), BF16),
                pltpu.VMEM((8, 2, 2, 64, 512), BF16),
                pltpu.VMEM((2, 128, 512), F32),
                dma((15,)),
                dma((16,)),
                dma((16,)),
                dma((8,)),
                dma((8,)),
                dma((16,)),
                dma((16,)),
                dma((12,)),
                dma((12,)),
                dma((10,)),
                dma((10,)),
                dma((28,)),
                dma((28,)),
                dma((3,)),
                dma((3,)),
            ],
            compiler_params=pltpu.CompilerParams(
                collective_id=0, has_side_effects=True, vmem_limit_bytes=60 * 1024 * 1024
            ),
        )(
            u_now,
            u_prev,
            buoyancy,
            modulus,
            station_cell.reshape(1, 128),
            path_class,
            spectra,
            cos_table,
            sin_table,
            path_filter,
    )
    return pl.pallas_call(
        merge,
        out_shape=(jax.ShapeDtypeStruct((128, 1024), F32), jax.ShapeDtypeStruct((128, 256), F32)),
        in_specs=[anywhere] * 6,
        out_specs=(anywhere,) * 2,
        scratch_shapes=[
            pltpu.VMEM((2, 128, 512), F32),
            pltpu.VMEM((8, 128), F32),
            pltpu.VMEM((4, 1024), F32),
            pltpu.VMEM((1, 512), F32),
            pltpu.VMEM((128, 1024), F32),
            pltpu.VMEM((128, 256), F32),
            dma((8,)),
        ],
        compiler_params=pltpu.CompilerParams(vmem_limit_bytes=60 * 1024 * 1024),
    )(mine, other, samples, field, lf_basis, crossover.reshape(1, 512))


def solution(mesh):
    in_specs = (
        P("grid", "sta"),
        P("grid", "sta"),
        P("grid", "sta"),
        P("grid", "sta"),
        P(("grid", "sta")),
        P(("grid", "sta"), None),
        P("sta", None),
        P("sta", None),
        P("sta", None),
        P(),
        P(),
        P(),
    )
    out_specs = (P(("grid", "sta"), None), P("grid", "sta"))
    return jax.shard_map(local, mesh=mesh, in_specs=in_specs, out_specs=out_specs, check_vma=False)
```

time: 38.3 us -> 35.2 us (0.919)
  local copies, waits for them, and re-layouts: 2.58 us -> 0 us
  Pallas kernels: 35 us -> 34.5 us
    unnamed x4 -> x0, local copies, waits for them, and re-layouts: 2.58 us -> none
    pallas_call x1 -> x2, Pallas kernels: 35 us -> 34.5 us  [the longest x1 32.3 us: local(): pl.pallas_call(kernel, out_shape=(jax.ShapeDtypeStruct((128, 512), F32),...]
where the time goes in v3:
time: 35.2 us; the launch traced here: 35.1 us
  Pallas kernels  34.5 us (98%)
  between operations  0.64 us (2%)
    pallas_call x1, Pallas kernels, local(): pl.pallas_call(kernel, out_shape=(jax.ShapeDtypeStruct((128, 512), F32),...  32.3 us
    pallas_call x1, Pallas kernels, local(): pl.pallas_call(merge, out_shape=(jax.ShapeDtypeStruct((128, 1024), F32),...  2.18 us

profile of v3, /device:TPU:1, one launch (start us, length us, event | category | flops | bytes accessed | tf_op | source)
XLA Modules:
  0.0 35.1 jit_solution(2736545624927195729)
XLA Ops:
  0.6 32.3 %shard_map.131 = (f32[128,512]{1,0:T(8,128)}, f32[128,512]{1,0:T(8,128)}, f32[8,128]{1,0:T(8,128)}, f32[128,256]{1,0:T(8,128)}) custom-call(f32[128,256]{1,0:T(8,128)} %u_ref.1, f32[128,256]{1,0:T(8,128)} %up_ref.1, f32[128,256]{1,0:T(8,128)} %b_ref.1, f32[128,256]{1,0:T(8,128)} %m_ref.1, s32[1,128]{1,0:T(1,128)} %bitcast.3, s32[128,2048]{1,0:T(8,128)} %class_ref.1, ...), custom_call_target="tpu_custom_call" | custom-call | tf_op jit(solution)/shard_map/pallas_call | solution.py:469
  32.9 2.2 %shard_map.132 = (f32[128,1024]{1,0:T(8,128)}, f32[128,256]{1,0:T(8,128)}) custom-call(f32[128,512]{1,0:T(8,128)} %get-tuple-element.6.mine_ref, f32[128,512]{1,0:T(8,128)} %get-tuple-element.7.other_ref, f32[8,128]{1,0:T(8,128)} %get-tuple-element.8.samples_ref, f32[128,256]{1,0:T(8,128)} %get-tuple-element.9.field_ref, f32[4,1024]{1,0:T(4,128)} %basis_ref.1, ...), custom_call_target="tpu_custom_call" | custom-call | tf_op jit(solution)/shard_map/pallas_call | solution.py:535

commit v4 on v3

--- a/solution.py
+++ b/solution.py
@@ -16,6 +16,7 @@
 SLOTS = ((0, 0), (0, 1), (1, 0), (3, 0), (1, 1), (3, 1), (2, 0), (2, 1))
 SIDES = [(0, -1), (0, 1), (-1, -1), (-1, 1), (1, -1), (1, 1)]
 HALO = [(-1, 0), (1, 0)] + SIDES
+FORWARDED = ((6, 0, 0), (6, 0, 1), (5, 0, 0), (4, 0, 1))
 GRID = 16
 FARTHEST = (8, 9, 7, 10, 6, 11, 5, 12, 4, 13, 3, 14, 2, 15, 1, 0)
 SUBCHIP = 256
@@ -132,6 +133,19 @@
         packed = jnp.where(lane // 8 == a, pltpu.roll(both, 8 * a + 4, 1), packed)
     colsrc[...] = jnp.transpose(packed)[0:32].reshape(4, 8, 128)
 
+    load_class.wait()
+    for slot, (dy, cross) in enumerate(SLOTS):
+        source = ((y + dy) % 4) * 2 + (xh + cross) % 2
+        columns = pl.ds(pl.multiple_of(source * SUBCHIP, SUBCHIP), SUBCHIP)
+        classown[:, slot * SUBCHIP : (slot + 1) * SUBCHIP] = classraw[:, columns].astype(F32).astype(BF16)
+    def expand(which, classes):
+        held = classes[...]
+        for c in range(1, CLASSES):
+            onehot[which, (c - 1) * 128 : c * 128, :] = jnp.where(held == BF16(c), BF16(1), BF16(0))
+        onehot[which, 896:912, :] = jnp.ones((16, 2048), BF16)
+
+    expand(0, classown)
+
     pl.semaphore_wait(barrier, len(partners))
 
     def remote(src, dst, send, recv, target):
@@ -153,9 +167,11 @@
             half = 1 if ds == 1 else 0
             src, dst = ext.at[:, rows, pl.ds(half * 128, 128)], cornerin.at[side * 2 + half]
         halo_copies.append(remote(src, dst, halo_send.at[i], halo_recv.at[i], beside(dg, ds)))
-    cell_copies = [
-        remote(cellsrc, cells.at[GRID - r], cell_send.at[r], cell_recv.at[r], along_grid(r)) for r in FARTHEST if r
-    ]
+    cell_copies = {
+        GRID - r: remote(cellsrc, cells.at[GRID - r], cell_send.at[r], cell_recv.at[r], along_grid(r))
+        for r in FARTHEST
+        if r
+    }
     near_copies = {}
 
     def send_near(turn):
@@ -196,49 +212,27 @@
             i = (slot - 1) * 4 + quarter
             plane_copies[slot, quarter] = remote(rows, rows, plane_send.at[i], plane_recv.at[i], plane[i % 3])
 
-    load_class.wait()
-    for slot, (dy, cross) in enumerate(SLOTS):
-        source = ((y + dy) % 4) * 2 + (xh + cross) % 2
-        columns = pl.ds(pl.multiple_of(source * SUBCHIP, SUBCHIP), SUBCHIP)
-        classown[:, slot * SUBCHIP : (slot + 1) * SUBCHIP] = classraw[:, columns].astype(F32).astype(BF16)
     sib_class = remote(classown, classsib, sib_send.at[1], sib_recv.at[1], sibling)
     pieces[0, core] = phased[core]
     cells[0] = cellsrc[...]
 
-    def expand(which, classes):
-        held = classes[...]
-        for c in range(1, CLASSES):
-            onehot[which, (c - 1) * 128 : c * 128, :] = jnp.where(held == BF16(c), BF16(1), BF16(0))
-        onehot[which, 896:912, :] = jnp.ones((16, 2048), BF16)
-
-    expand(0, classown)
+    sib_piece.wait_recv()
     send_near(1)
     sib_class.wait_recv()
     expand(1, classsib)
     load_filter.wait()
 
-    def multiply(slot):
-        for quarter in range(4) if 0 < slot < 7 else ():
-            plane_copies[slot, quarter].wait_recv()
-        part = pl.ds(slot * SUBCHIP, SUBCHIP)
-        for n in (0, 256):
-            weights = pieces[slot, :, :, :, n : n + 256].reshape(SUBCHIP, 256)
-            first = filters[0:1, n : n + 256]
-            total = jnp.dot(onehot[0, 896:912, part], weights, preferred_element_type=F32)
-            acc = first * total[0:1]
-            for c in range(1, CLASSES):
-                lhs = onehot[:, (c - 1) * 128 : c * 128, part].reshape(256, SUBCHIP)
-                acc = acc + (filters[c : c + 1, n : n + 256] - first) * jnp.dot(
-                    lhs, weights, preferred_element_type=F32
-                )
-            acc = acc.reshape(2, 128, 256)
-            if slot == 0:
-                high[:, :, n : n + 256] = acc
-            else:
-                high[:, :, n : n + 256] += acc
-
-    sib_piece.wait_recv()
-    multiply(0)
+    def arrived(dy, cross, part):
+        for dc in (0, 1):
+            near_copies[dy, cross, dc, part].wait_recv()
+
+    for copy in ((1, 0, 0), (3, 0, 1), (0, 1, 0)):
+        arrived(*copy)
+    relay(3, 1, 0, 6, 0)
+    relay(2, 3, 0, 6, 1)
+    share(3, 0, colour)
+    share(2, 1, colour)
+    share(1, 0, colour)
 
     for copy in halo_copies:
         copy.wait_recv()
@@ -292,17 +286,6 @@
     field_out = pltpu.make_async_copy(final, field_ref, load_sem.at[13])
     field_out.start()
 
-    def arrived(dy, cross, part):
-        for dc in (0, 1):
-            near_copies[dy, cross, dc, part].wait_recv()
-
-    for copy in ((1, 0, 0), (3, 0, 1), (0, 1, 0)):
-        arrived(*copy)
-    relay(3, 1, 0, 6, 0)
-    relay(2, 3, 0, 6, 1)
-    share(3, 0, colour)
-    share(2, 1, colour)
-    share(1, 0, colour)
     for copy in ((1, 0, 1), (3, 0, 0), (0, 1, 1)):
         arrived(*copy)
     relay(1, 1, 0, 5, 0)
@@ -313,13 +296,49 @@
     share(3, 1, colour)
     share(2, 0, colour)
 
-    for copy in cell_copies:
-        copy.wait_recv()
+    results, stores = [], []
+
+    def multiply(slot):
+        for quarter in range(4):
+            if (slot, quarter) in plane_copies:
+                plane_copies[slot, quarter].wait_recv()
+        for cross, part in ((0, 0), (0, 1), (1, 0), (1, 1)):
+            if (slot, cross, part) in relay_copies and (slot, cross, part) not in FORWARDED:
+                relay_copies[slot, cross, part].wait_recv()
+        part = pl.ds(slot * SUBCHIP, SUBCHIP)
+        for n in (0, 256):
+            weights = pieces[slot, :, :, :, n : n + 256].reshape(SUBCHIP, 256)
+            first = filters[0:1, n : n + 256]
+            total = jnp.dot(onehot[0, 896:912, part], weights, preferred_element_type=F32)
+            acc = first * total[0:1]
+            for c in range(1, CLASSES):
+                lhs = onehot[:, (c - 1) * 128 : c * 128, part].reshape(256, SUBCHIP)
+                acc = acc + (filters[c : c + 1, n : n + 256] - first) * jnp.dot(
+                    lhs, weights, preferred_element_type=F32
+                )
+            acc = acc.reshape(2, 128, 256)
+            if slot == 0:
+                high[:, :, n : n + 256] = acc
+            else:
+                high[:, :, n : n + 256] += acc
+            if slot == 7:
+                done = pl.ds(n, 256)
+                i = 2 + n // 256
+                results.append(
+                    remote(high.at[1, :, done], other_ref.at[:, done], sib_send.at[i], sib_recv.at[i], sibling)
+                )
+                mine_out = pltpu.make_async_copy(high.at[0, :, done], mine_ref.at[:, done], load_sem.at[13 + i])
+                mine_out.start()
+                stores.append(mine_out)
+
     row_at = lax.broadcasted_iota(jnp.int32, (128, 128), 0)
     col_at = lax.broadcasted_iota(jnp.int32, (256, 128), 0)
     samp_copies = []
     for pair in range(0, GRID, 2):
-        pair = FARTHEST[pair : pair + 2]
+        pair = FARTHEST[14 - pair : 16 - pair]
+        for r in pair:
+            if r > 0:
+                cell_copies[r].wait_recv()
         picks, inside = [], []
         for r in pair:
             cell = cells[r, 0:1, :]
@@ -344,6 +363,9 @@
                     remote(sampsrc.at[r], sampin.at[GRID - r], samp_send.at[r], samp_recv.at[r], along_grid(r))
                 )
 
+    relay(1, 1, 0, 5, 1)
+    relay(1, 3, 0, 4, 0)
+    multiply(0)
     relay_copies[6, 0, 0].wait_recv()
     relay_copies[6, 0, 1].wait_recv()
     relay(6, 0, 1, 7, 0)
@@ -356,23 +378,9 @@
     relay(4, 3, 0, 7, 1)
     share(5, 0, colour)
     share(4, 1, colour)
-    multiply(1)
-    relay_copies[5, 1, 1].wait_recv()
-    relay_copies[4, 1, 0].wait_recv()
-    share(5, 1, 1 - colour)
-    share(4, 0, 1 - colour)
-    for slot in (2, 3, 6):
+    for slot in (1, 2, 3, 6, 5, 4, 7):
         multiply(slot)
-    for cross in (0, 1):
-        for part in (0, 1):
-            relay_copies[7, cross, part].wait_recv()
-    multiply(7)
-    multiply(4)
-    multiply(5)
-
-    sib_high = remote(high.at[1], other_ref, sib_send.at[2], sib_recv.at[2], sibling)
-    mine_out = pltpu.make_async_copy(high.at[0], mine_ref, load_sem.at[12])
-    mine_out.start()
+
     for copy in samp_copies:
         copy.wait_recv()
     samples = sampsrc[0]
@@ -381,14 +389,16 @@
     total_samples[...] = samples
     samples_out = pltpu.make_async_copy(total_samples, samples_ref, load_sem.at[14])
     samples_out.start()
-    sib_high.wait_recv()
-    mine_out.wait()
+    for copy in results:
+        copy.wait_recv()
+    for copy in stores:
+        copy.wait()
     samples_out.wait()
     field_out.wait()
 
-    sent = halo_copies + cell_copies + samp_copies + list(near_copies.values()) + list(relay_copies.values())
+    sent = halo_copies + list(cell_copies.values()) + samp_copies + list(near_copies.values()) + list(relay_copies.values())
     sent += list(plane_copies.values())
-    for copy in sent + [sib_piece, sib_class, sib_high]:
+    for copy in sent + [sib_piece, sib_class] + results:
         copy.wait_send()
 
 
@@ -501,7 +511,7 @@
                 pltpu.VMEM((2, 2, 64, 512), BF16),
                 pltpu.VMEM((8, 2, 2, 64, 512), BF16),
                 pltpu.VMEM((2, 128, 512), F32),
-                dma((15,)),
+                dma((17,)),
                 dma((16,)),
                 dma((16,)),
                 dma((8,)),
@@ -510,12 +520,12 @@
                 dma((16,)),
                 dma((12,)),
                 dma((12,)),
-                dma((10,)),
-                dma((10,)),
+                dma((12,)),
+                dma((12,)),
                 dma((28,)),
                 dma((28,)),
-                dma((3,)),
-                dma((3,)),
+                dma((4,)),
+                dma((4,)),
             ],
             compiler_params=pltpu.CompilerParams(
                 collective_id=0, has_side_effects=True, vmem_limit_bytes=60 * 1024 * 1024

time: 35.2 us -> 34.2 us (0.972)
  Pallas kernels: 34.5 us -> 33.4 us
    pallas_call x1, Pallas kernels: 32.3 us -> 31.3 us  [local(): pl.pallas_call(kernel, out_shape=(jax.ShapeDtypeStruct((128, 512), F32),...]
where the time goes in v4:
time: 34.2 us; the launch traced here: 34.1 us
  Pallas kernels  33.4 us (98%)
  between operations  0.64 us (2%)
    pallas_call x1, Pallas kernels, local(): pl.pallas_call(kernel, out_shape=(jax.ShapeDtypeStruct((128, 512), F32),...  31.3 us
    pallas_call x1, Pallas kernels, local(): pl.pallas_call(merge, out_shape=(jax.ShapeDtypeStruct((128, 1024), F32),...  2.18 us

profile of v4, /device:TPU:1, one launch (start us, length us, event | category | flops | bytes accessed | tf_op | source)
XLA Modules:
  0.0 34.1 jit_solution(5412573793632826616)
XLA Ops:
  0.6 31.3 %shard_map.131 = (f32[128,512]{1,0:T(8,128)}, f32[128,512]{1,0:T(8,128)}, f32[8,128]{1,0:T(8,128)}, f32[128,256]{1,0:T(8,128)}) custom-call(f32[128,256]{1,0:T(8,128)} %u_ref.1, f32[128,256]{1,0:T(8,128)} %up_ref.1, f32[128,256]{1,0:T(8,128)} %b_ref.1, f32[128,256]{1,0:T(8,128)} %m_ref.1, s32[1,128]{1,0:T(1,128)} %bitcast.3, s32[128,2048]{1,0:T(8,128)} %class_ref.1, ...), custom_call_target="tpu_custom_call" | custom-call | tf_op jit(solution)/shard_map/pallas_call | solution.py:479
  31.9 2.2 %shard_map.132 = (f32[128,1024]{1,0:T(8,128)}, f32[128,256]{1,0:T(8,128)}) custom-call(f32[128,512]{1,0:T(8,128)} %get-tuple-element.6.mine_ref, f32[128,512]{1,0:T(8,128)} %get-tuple-element.7.other_ref, f32[8,128]{1,0:T(8,128)} %get-tuple-element.8.samples_ref, f32[128,256]{1,0:T(8,128)} %get-tuple-element.9.field_ref, f32[4,1024]{1,0:T(4,128)} %basis_ref.1, ...), custom_call_target="tpu_custom_call" | custom-call | tf_op jit(solution)/shard_map/pallas_call | solution.py:545

commit v5 on v4

--- a/solution.py
+++ b/solution.py
@@ -17,6 +17,7 @@
 SIDES = [(0, -1), (0, 1), (-1, -1), (-1, 1), (1, -1), (1, 1)]
 HALO = [(-1, 0), (1, 0)] + SIDES
 FORWARDED = ((6, 0, 0), (6, 0, 1), (5, 0, 0), (4, 0, 1))
+TILT = (0, 0, 2, 1, 0, 2, 0, 0)
 GRID = 16
 FARTHEST = (8, 9, 7, 10, 6, 11, 5, 12, 4, 13, 3, 14, 2, 15, 1, 0)
 SUBCHIP = 256
@@ -133,18 +134,12 @@
         packed = jnp.where(lane // 8 == a, pltpu.roll(both, 8 * a + 4, 1), packed)
     colsrc[...] = jnp.transpose(packed)[0:32].reshape(4, 8, 128)
 
-    load_class.wait()
-    for slot, (dy, cross) in enumerate(SLOTS):
-        source = ((y + dy) % 4) * 2 + (xh + cross) % 2
-        columns = pl.ds(pl.multiple_of(source * SUBCHIP, SUBCHIP), SUBCHIP)
-        classown[:, slot * SUBCHIP : (slot + 1) * SUBCHIP] = classraw[:, columns].astype(F32).astype(BF16)
     def expand(which, classes):
         held = classes[...]
         for c in range(1, CLASSES):
             onehot[which, (c - 1) * 128 : c * 128, :] = jnp.where(held == BF16(c), BF16(1), BF16(0))
         onehot[which, 896:912, :] = jnp.ones((16, 2048), BF16)
 
-    expand(0, classown)
 
     pl.semaphore_wait(barrier, len(partners))
 
@@ -210,9 +205,15 @@
         for quarter in (2 * part, 2 * part + 1):
             rows = pieces.at[slot, :, half, pl.ds(16 * quarter, 16)]
             i = (slot - 1) * 4 + quarter
-            plane_copies[slot, quarter] = remote(rows, rows, plane_send.at[i], plane_recv.at[i], plane[i % 3])
-
+            plane_copies[slot, quarter] = remote(rows, rows, plane_send.at[i], plane_recv.at[i], plane[(i + TILT[slot]) % 3])
+
+    load_class.wait()
+    for slot, (dy, cross) in enumerate(SLOTS):
+        source = ((y + dy) % 4) * 2 + (xh + cross) % 2
+        columns = pl.ds(pl.multiple_of(source * SUBCHIP, SUBCHIP), SUBCHIP)
+        classown[:, slot * SUBCHIP : (slot + 1) * SUBCHIP] = classraw[:, columns].astype(F32).astype(BF16)
     sib_class = remote(classown, classsib, sib_send.at[1], sib_recv.at[1], sibling)
+    expand(0, classown)
     pieces[0, core] = phased[core]
     cells[0] = cellsrc[...]
 
@@ -221,6 +222,43 @@
     sib_class.wait_recv()
     expand(1, classsib)
     load_filter.wait()
+
+    results, stores = [], []
+
+    def multiply(slot):
+        for quarter in range(4):
+            if (slot, quarter) in plane_copies:
+                plane_copies[slot, quarter].wait_recv()
+        for cross, part in ((0, 0), (0, 1), (1, 0), (1, 1)):
+            if (slot, cross, part) in relay_copies and (slot, cross, part) not in FORWARDED:
+                relay_copies[slot, cross, part].wait_recv()
+        part = pl.ds(slot * SUBCHIP, SUBCHIP)
+        for n in (0, 256):
+            weights = pieces[slot, :, :, :, n : n + 256].reshape(SUBCHIP, 256)
+            first = filters[0:1, n : n + 256]
+            total = jnp.dot(onehot[0, 896:912, part], weights, preferred_element_type=F32)
+            acc = first * total[0:1]
+            for c in range(1, CLASSES):
+                lhs = onehot[:, (c - 1) * 128 : c * 128, part].reshape(256, SUBCHIP)
+                acc = acc + (filters[c : c + 1, n : n + 256] - first) * jnp.dot(
+                    lhs, weights, preferred_element_type=F32
+                )
+            acc = acc.reshape(2, 128, 256)
+            if slot == 0:
+                high[:, :, n : n + 256] = acc
+            else:
+                high[:, :, n : n + 256] += acc
+            if slot == 7:
+                done = pl.ds(n, 256)
+                i = 2 + n // 256
+                results.append(
+                    remote(high.at[1, :, done], other_ref.at[:, done], sib_send.at[i], sib_recv.at[i], sibling)
+                )
+                mine_out = pltpu.make_async_copy(high.at[0, :, done], mine_ref.at[:, done], load_sem.at[13 + i])
+                mine_out.start()
+                stores.append(mine_out)
+
+    multiply(0)
 
     def arrived(dy, cross, part):
         for dc in (0, 1):
@@ -296,41 +334,6 @@
     share(3, 1, colour)
     share(2, 0, colour)
 
-    results, stores = [], []
-
-    def multiply(slot):
-        for quarter in range(4):
-            if (slot, quarter) in plane_copies:
-                plane_copies[slot, quarter].wait_recv()
-        for cross, part in ((0, 0), (0, 1), (1, 0), (1, 1)):
-            if (slot, cross, part) in relay_copies and (slot, cross, part) not in FORWARDED:
-                relay_copies[slot, cross, part].wait_recv()
-        part = pl.ds(slot * SUBCHIP, SUBCHIP)
-        for n in (0, 256):
-            weights = pieces[slot, :, :, :, n : n + 256].reshape(SUBCHIP, 256)
-            first = filters[0:1, n : n + 256]
-            total = jnp.dot(onehot[0, 896:912, part], weights, preferred_element_type=F32)
-            acc = first * total[0:1]
-            for c in range(1, CLASSES):
-                lhs = onehot[:, (c - 1) * 128 : c * 128, part].reshape(256, SUBCHIP)
-                acc = acc + (filters[c : c + 1, n : n + 256] - first) * jnp.dot(
-                    lhs, weights, preferred_element_type=F32
-                )
-            acc = acc.reshape(2, 128, 256)
-            if slot == 0:
-                high[:, :, n : n + 256] = acc
-            else:
-                high[:, :, n : n + 256] += acc
-            if slot == 7:
-                done = pl.ds(n, 256)
-                i = 2 + n // 256
-                results.append(
-                    remote(high.at[1, :, done], other_ref.at[:, done], sib_send.at[i], sib_recv.at[i], sibling)
-                )
-                mine_out = pltpu.make_async_copy(high.at[0, :, done], mine_ref.at[:, done], load_sem.at[13 + i])
-                mine_out.start()
-                stores.append(mine_out)
-
     row_at = lax.broadcasted_iota(jnp.int32, (128, 128), 0)
     col_at = lax.broadcasted_iota(jnp.int32, (256, 128), 0)
     samp_copies = []
@@ -365,7 +368,6 @@
 
     relay(1, 1, 0, 5, 1)
     relay(1, 3, 0, 4, 0)
-    multiply(0)
     relay_copies[6, 0, 0].wait_recv()
     relay_copies[6, 0, 1].wait_recv()
     relay(6, 0, 1, 7, 0)

time: 34.2 us -> 33.8 us (0.988)
  Pallas kernels: 33.4 us -> 33 us
    pallas_call x1, Pallas kernels: 31.3 us -> 30.8 us  [local(): pl.pallas_call(kernel, out_shape=(jax.ShapeDtypeStruct((128, 512), F32),...]
where the time goes in v5:
time: 33.8 us; the launch traced here: 33.6 us
  Pallas kernels  33 us (98%)
  between operations  0.64 us (2%)
    pallas_call x1, Pallas kernels, local(): pl.pallas_call(kernel, out_shape=(jax.ShapeDtypeStruct((128, 512), F32),...  30.8 us
    pallas_call x1, Pallas kernels, local(): pl.pallas_call(merge, out_shape=(jax.ShapeDtypeStruct((128, 1024), F32),...  2.18 us

profile of v5, /device:TPU:1, one launch (start us, length us, event | category | flops | bytes accessed | tf_op | source)
XLA Modules:
  0.0 33.6 jit_solution(15415309944103291031)
XLA Ops:
  0.6 30.8 %shard_map.131 = (f32[128,512]{1,0:T(8,128)}, f32[128,512]{1,0:T(8,128)}, f32[8,128]{1,0:T(8,128)}, f32[128,256]{1,0:T(8,128)}) custom-call(f32[128,256]{1,0:T(8,128)} %u_ref.1, f32[128,256]{1,0:T(8,128)} %up_ref.1, f32[128,256]{1,0:T(8,128)} %b_ref.1, f32[128,256]{1,0:T(8,128)} %m_ref.1, s32[1,128]{1,0:T(1,128)} %bitcast.3, s32[128,2048]{1,0:T(8,128)} %class_ref.1, ...), custom_call_target="tpu_custom_call" | custom-call | tf_op jit(solution)/shard_map/pallas_call | solution.py:481
  31.4 2.2 %shard_map.132 = (f32[128,1024]{1,0:T(8,128)}, f32[128,256]{1,0:T(8,128)}) custom-call(f32[128,512]{1,0:T(8,128)} %get-tuple-element.6.mine_ref, f32[128,512]{1,0:T(8,128)} %get-tuple-element.7.other_ref, f32[8,128]{1,0:T(8,128)} %get-tuple-element.8.samples_ref, f32[128,256]{1,0:T(8,128)} %get-tuple-element.9.field_ref, f32[4,1024]{1,0:T(4,128)} %basis_ref.1, ...), custom_call_target="tpu_custom_call" | custom-call | tf_op jit(solution)/shard_map/pallas_call | solution.py:547

commit v6 on v5

--- a/solution.py
+++ b/solution.py
@@ -337,34 +337,38 @@
     row_at = lax.broadcasted_iota(jnp.int32, (128, 128), 0)
     col_at = lax.broadcasted_iota(jnp.int32, (256, 128), 0)
     samp_copies = []
-    for pair in range(0, GRID, 2):
-        pair = FARTHEST[14 - pair : 16 - pair]
-        for r in pair:
-            if r > 0:
-                cell_copies[r].wait_recv()
-        picks, inside = [], []
-        for r in pair:
-            cell = cells[r, 0:1, :]
-            row = lax.shift_right_logical(cell, 12) - g * 128
-            col = lax.bitwise_and(cell, 4095) - s * 256
-            picks.append(jnp.where(col_at == col, F32(1), zero).astype(BF16))
-            inside.append(row_at == row)
-        found = jnp.dot(
-            ush[...].reshape(4 * 256, 256), jnp.concatenate(picks, axis=1), preferred_element_type=F32
-        )
-        mask = jnp.concatenate(inside, axis=1)
-        recorded = []
-        for step in range(STEPS):
-            both = found[step * 256 : step * 256 + 128] + found[step * 256 + 128 : step * 256 + 256]
-            recorded.append(jnp.sum(jnp.where(mask, both, zero), axis=0, keepdims=True))
-        recorded = jnp.concatenate(recorded + [jnp.zeros((4, 256), F32)], axis=0)
-        sampsrc[pair[0]] = recorded[:, 0:128]
-        sampsrc[pair[1]] = recorded[:, 128:256]
-        for r in pair:
-            if r > 0:
-                samp_copies.append(
-                    remote(sampsrc.at[r], sampin.at[GRID - r], samp_send.at[r], samp_recv.at[r], along_grid(r))
-                )
+
+    def look_up(first, last):
+        for pair in range(first, last, 2):
+            pair = FARTHEST[pair : pair + 2]
+            for r in pair:
+                if r > 0:
+                    cell_copies[r].wait_recv()
+            picks, inside = [], []
+            for r in pair:
+                cell = cells[r, 0:1, :]
+                row = lax.shift_right_logical(cell, 12) - g * 128
+                col = lax.bitwise_and(cell, 4095) - s * 256
+                picks.append(jnp.where(col_at == col, F32(1), zero).astype(BF16))
+                inside.append(row_at == row)
+            found = jnp.dot(
+                ush[...].reshape(4 * 256, 256), jnp.concatenate(picks, axis=1), preferred_element_type=F32
+            )
+            mask = jnp.concatenate(inside, axis=1)
+            recorded = []
+            for step in range(STEPS):
+                both = found[step * 256 : step * 256 + 128] + found[step * 256 + 128 : step * 256 + 256]
+                recorded.append(jnp.sum(jnp.where(mask, both, zero), axis=0, keepdims=True))
+            recorded = jnp.concatenate(recorded + [jnp.zeros((4, 256), F32)], axis=0)
+            sampsrc[pair[0]] = recorded[:, 0:128]
+            sampsrc[pair[1]] = recorded[:, 128:256]
+            for r in pair:
+                if r > 0:
+                    samp_copies.append(
+                        remote(sampsrc.at[r], sampin.at[GRID - r], samp_send.at[r], samp_recv.at[r], along_grid(r))
+                    )
+
+    look_up(0, GRID // 2)
 
     relay(1, 1, 0, 5, 1)
     relay(1, 3, 0, 4, 0)
@@ -374,6 +378,7 @@
     relay(6, 0, 1, 7, 1)
     share(6, 0, colour)
     share(6, 1, colour)
+    look_up(GRID // 2, GRID)
     relay_copies[5, 0, 0].wait_recv()
     relay(5, 1, 0, 7, 0)
     relay_copies[4, 0, 1].wait_recv()

time: 33.8 us -> 33.3 us (0.985)
  Pallas kernels: 33 us -> 32.6 us
    pallas_call x1, Pallas kernels: 30.8 us -> 30.4 us  [local(): pl.pallas_call(kernel, out_shape=(jax.ShapeDtypeStruct((128, 512), F32),...]
where the time goes in v6:
time: 33.3 us; the launch traced here: 33.2 us
  Pallas kernels  32.6 us (98%)
  between operations  0.64 us (2%)
    pallas_call x1, Pallas kernels, local(): pl.pallas_call(kernel, out_shape=(jax.ShapeDtypeStruct((128, 512), F32),...  30.4 us
    pallas_call x1, Pallas kernels, local(): pl.pallas_call(merge, out_shape=(jax.ShapeDtypeStruct((128, 1024), F32),...  2.18 us

profile of v6, /device:TPU:1, one launch (start us, length us, event | category | flops | bytes accessed | tf_op | source)
XLA Modules:
  0.0 33.2 jit_solution(18002256601813014940)
XLA Ops:
  0.6 30.4 %shard_map.131 = (f32[128,512]{1,0:T(8,128)}, f32[128,512]{1,0:T(8,128)}, f32[8,128]{1,0:T(8,128)}, f32[128,256]{1,0:T(8,128)}) custom-call(f32[128,256]{1,0:T(8,128)} %u_ref.1, f32[128,256]{1,0:T(8,128)} %up_ref.1, f32[128,256]{1,0:T(8,128)} %b_ref.1, f32[128,256]{1,0:T(8,128)} %m_ref.1, s32[1,128]{1,0:T(1,128)} %bitcast.3, s32[128,2048]{1,0:T(8,128)} %class_ref.1, ...), custom_call_target="tpu_custom_call" | custom-call | tf_op jit(solution)/shard_map/pallas_call | solution.py:486
  31.0 2.2 %shard_map.132 = (f32[128,1024]{1,0:T(8,128)}, f32[128,256]{1,0:T(8,128)}) custom-call(f32[128,512]{1,0:T(8,128)} %get-tuple-element.6.mine_ref, f32[128,512]{1,0:T(8,128)} %get-tuple-element.7.other_ref, f32[8,128]{1,0:T(8,128)} %get-tuple-element.8.samples_ref, f32[128,256]{1,0:T(8,128)} %get-tuple-element.9.field_ref, f32[4,1024]{1,0:T(4,128)} %basis_ref.1, ...), custom_call_target="tpu_custom_call" | custom-call | tf_op jit(solution)/shard_map/pallas_call | solution.py:552

commit v7 on v6

--- a/solution.py
+++ b/solution.py
@@ -264,10 +264,11 @@
         for dc in (0, 1):
             near_copies[dy, cross, dc, part].wait_recv()
 
-    for copy in ((1, 0, 0), (3, 0, 1), (0, 1, 0)):
-        arrived(*copy)
+    arrived(1, 0, 0)
     relay(3, 1, 0, 6, 0)
+    arrived(3, 0, 1)
     relay(2, 3, 0, 6, 1)
+    arrived(0, 1, 0)
     share(3, 0, colour)
     share(2, 1, colour)
     share(1, 0, colour)
@@ -373,8 +374,8 @@
     relay(1, 1, 0, 5, 1)
     relay(1, 3, 0, 4, 0)
     relay_copies[6, 0, 0].wait_recv()
+    relay(6, 0, 1, 7, 0)
     relay_copies[6, 0, 1].wait_recv()
-    relay(6, 0, 1, 7, 0)
     relay(6, 0, 1, 7, 1)
     share(6, 0, colour)
     share(6, 1, colour)

time: 33.3 us -> 33.3 us (level)
  no operation moved by 1% of the time
where the time goes in v7:
time: 33.3 us; the launch traced here: 33.1 us
  Pallas kernels  32.5 us (98%)
  between operations  0.64 us (2%)
    pallas_call x1, Pallas kernels, local(): pl.pallas_call(kernel, out_shape=(jax.ShapeDtypeStruct((128, 512), F32),...  30.3 us
    pallas_call x1, Pallas kernels, local(): pl.pallas_call(merge, out_shape=(jax.ShapeDtypeStruct((128, 1024), F32),...  2.18 us

profile of v7, /device:TPU:1, one launch (start us, length us, event | category | flops | bytes accessed | tf_op | source)
XLA Modules:
  0.0 33.1 jit_solution(3551455929976698187)
XLA Ops:
  0.6 30.3 %shard_map.131 = (f32[128,512]{1,0:T(8,128)}, f32[128,512]{1,0:T(8,128)}, f32[8,128]{1,0:T(8,128)}, f32[128,256]{1,0:T(8,128)}) custom-call(f32[128,256]{1,0:T(8,128)} %u_ref.1, f32[128,256]{1,0:T(8,128)} %up_ref.1, f32[128,256]{1,0:T(8,128)} %b_ref.1, f32[128,256]{1,0:T(8,128)} %m_ref.1, s32[1,128]{1,0:T(1,128)} %bitcast.3, s32[128,2048]{1,0:T(8,128)} %class_ref.1, ...), custom_call_target="tpu_custom_call" | custom-call | tf_op jit(solution)/shard_map/pallas_call | solution.py:487
  31.0 2.2 %shard_map.132 = (f32[128,1024]{1,0:T(8,128)}, f32[128,256]{1,0:T(8,128)}) custom-call(f32[128,512]{1,0:T(8,128)} %get-tuple-element.6.mine_ref, f32[128,512]{1,0:T(8,128)} %get-tuple-element.7.other_ref, f32[8,128]{1,0:T(8,128)} %get-tuple-element.8.samples_ref, f32[128,256]{1,0:T(8,128)} %get-tuple-element.9.field_ref, f32[4,1024]{1,0:T(4,128)} %basis_ref.1, ...), custom_call_target="tpu_custom_call" | custom-call | tf_op jit(solution)/shard_map/pallas_call | solution.py:553
